TPU v7x, 128 devices: a whole 4x4x4 slice. The times are simulated.
128 devices in a mesh: aux: 16 (over y, x), orb: 8 (over z, core).
Axes of the slice: x: 4, y: 4, z: 4, core: 2. Of those that a mesh axis runs over, the one named last changes fastest.
Arguments:
- integrals: bfloat16 [256, 64, 16384], P(('aux', 'orb')), may hold values from -0.75 to 0.75
- tile_mu: int32 [256], P(('aux', 'orb')), may hold values from 0 to 31
- tile_nu: int32 [256], P(('aux', 'orb')), may hold values from 0 to 31
- live_count: int32 [128], P(('aux', 'orb')), may hold values from 1 to 2, as said below
- support: int32 [64, 16], replicated, may hold values from 0 to 31, as said below
- coeffs: bfloat16 [64, 1024], replicated, may hold values from -0.75 to 0.75
- pair_mu: int32 [512], replicated, may hold values from 0 to 31, as said below
- pair_nu: int32 [512], replicated, may hold values from 0 to 31
Outputs:
- exchange: float32 [512, 4096], P(('aux', 'orb'))
Inputs may be any that keep to these rules, and one draw needn't show every extreme that they name: A device's live integral slots are its first live_count ones; some device has all 2 live. An orbital's 16 support tiles are distinct. The pairs (pair_mu, pair_nu) are distinct and pair_mu != pair_nu.
All inputs are finite; a program needn't handle non-finite values.
Results may differ from a plain program's by a relative error of at most 0.004.
Values may be sent and summed in bfloat16 or wider, within the bound.
A program may use at most 128 MiB of HBM per device.

v0:
```python
import jax
import jax.numpy as jnp
from jax import lax
from jax.sharding import PartitionSpec as P

TILE = 64
AUX_DEV = 256
OCC = 64
SUP = 16
WT = 32


def coefficients(support, coeffs):
    onehot = (support[:, :, None] == jnp.arange(WT, dtype=jnp.int32)[None, None, :]).astype(
        jnp.float32
    )
    blocks = coeffs.reshape(OCC, SUP, TILE).astype(jnp.float32)
    table = jnp.einsum("osw,osn->wno", onehot, blocks, precision=lax.Precision.HIGHEST)
    return table.astype(jnp.bfloat16)


def tile_sums(tile_ids, products):
    onehot = (jnp.arange(WT, dtype=jnp.int32)[:, None] == tile_ids[None, :]).astype(jnp.float32)
    return jnp.dot(onehot, products.reshape(products.shape[0], -1), precision=lax.Precision.HIGHEST)


def on_device(integrals, tile_mu, tile_nu, live_count, support, coeffs, pair_mu, pair_nu):
    coeff_table = coefficients(support, coeffs)
    slot_count = integrals.shape[0]
    group = OCC // lax.axis_size("orb")
    slot_index = jnp.arange(slot_count, dtype=jnp.int32)
    live_rows = (slot_index < live_count[0]).astype(jnp.float32)
    picked = coeff_table[tile_nu]
    products = jnp.einsum("kni,knx->kix", picked, integrals, preferred_element_type=jnp.float32)
    products = products * live_rows[:, None, None]
    received = lax.all_to_all(products, "orb", split_axis=1, concat_axis=0, tiled=True)
    all_mu = lax.all_gather(tile_mu, "orb", axis=0, tiled=True)
    summed = tile_sums(all_mu, received)
    halves = summed.reshape(WT, group, AUX_DEV, TILE).transpose(0, 3, 1, 2)
    halves = halves.reshape(WT * TILE, group * AUX_DEV).astype(jnp.bfloat16)
    gram = jnp.dot(halves, halves.T, preferred_element_type=jnp.float32).reshape(WT, TILE, WT, TILE)
    total_pairs = pair_mu.shape[0]
    blocks = gram[pair_mu, :, pair_nu, :]
    return lax.psum_scatter(
        blocks.reshape(
            lax.axis_size(("aux", "orb"))
            * (total_pairs // (lax.axis_size("aux") * lax.axis_size("orb"))),
            TILE * TILE,
        ),
        ("aux", "orb"),
        scatter_dimension=0,
        tiled=True,
    )


def solution(mesh):
    return jax.shard_map(
        on_device,
        mesh=mesh,
        in_specs=(
            P(("aux", "orb"), None, None),
            P(("aux", "orb")),
            P(("aux", "orb")),
            P(("aux", "orb")),
            P(),
            P(),
            P(),
            P(),
        ),
        out_specs=P(("aux", "orb"), None),
        check_vma=False,
    )
```

profile of v0, /device:TPU:0, one launch (start us, length us, event | category | flops | bytes accessed | tf_op | source)
XLA Modules:
  0.0 443.1 jit_solution(15164370835303593812)
XLA Ops:
  6.5 1.1 reshape.27
  7.7 0.8 copy.15
  8.4 0.6 fusion.3
  9.1 0.6 copy.16
  9.7 0.7 compare_select_fusion.2
  11.0 0.6 gather_fusion
  11.6 3.5 convolution_multiply_fusion
  15.1 7.8 %copy.18 = f32[2,64,16384]{2,0,1:T(2,128)} copy(f32[2,64,16384]{2,1,0:T(8,128)S(1)} %convolution_multiply_fusion) | data formatting | bytes 16777216 | tf_op jit(solution)/shard_map/mul | solution.py:35
  22.9 0.0 copy-start.3
  22.9 0.0 copy-start.2
  22.9 0.0 copy-start
  22.9 0.0 copy-start.1
  22.9 5.5 %all-to-all-start = ((f32[2,64,16384]{2,0,1:T(2,128)}), f32[2,64,16384]{2,0,1:T(2,128)}, u32[]{:S(2)}, u32[]{:S(2)}) async-start(f32[2,64,16384]{2,0,1:T(2,128)} %copy.18), calls=%async_computation | async-start | bytes 16777216 | tf_op jit(solution)/shard_map/all_to_all | solution.py:36
  28.5 0.0 all-reduce.4.cloned.1.call-start
  28.5 0.0 copy-done.3
  28.5 0.6 dynamic-slice
  29.8 0.0 copy-done.2
  29.8 0.2 dynamic-update-slice
  30.0 95.9 %all-reduce = s32[16]{0:T(128)S(1)} all-reduce(s32[16]{0:T(128)S(1)} %dynamic-update-slice), channel_id=1, replica_groups=mesh['aux'=16,'orb'=8] {'orb'}, use_global_device_ids=true, to_apply=%add | all-reduce | flops 16 | bytes 128
  126.0 0.0 copy-done
  126.0 0.0 copy-done.1
  126.0 0.0 all-to-all-done
  126.0 8.1 %copy.19 = f32[2,8,8,16384]{3,2,0,1:T(8,128)S(1)} copy(f32[2,8,8,16384]{3,0,2,1:T(2,128)} %bitcast.5) | data formatting | bytes 16777216 | tf_op jit(solution)/shard_map/all_to_all | solution.py:36
  134.1 8.1 %copy.33 = f32[2,8,8,16384]{3,1,2,0:T(8,128)} copy(f32[2,8,8,16384]{3,2,1,0:T(8,128)S(1)} %bitcast.37) | data formatting | bytes 16777216
  142.2 17.4 %dot_general.19 = f32[8,256,64,16]{2,1,0,3:T(8,128)} reshape(f32[131072,16]{0,1:T(8,128)} %bitcast.36) | data formatting | bytes 16777216 | tf_op jit(solution)/shard_map/dot_general | solution.py:24
  159.6 13.6 %copy.20 = f32[8,256,64,16]{1,3,2,0:T(8,128)} copy(f32[8,256,64,16]{2,1,0,3:T(8,128)} %dot_general.19) | data formatting | bytes 16777216 | tf_op jit(solution)/shard_map/dot_general | solution.py:24
  173.2 11.7 %convolution_convert_fusion = bf16[32,8,256,64]{2,0,3,1:T(8,128)(2,1)} fusion(f32[8,256,64,16]{1,3,2,0:T(8,128)} %copy.20, s32[16]{0:T(128)S(1)} %all-reduce), kind=kOutput, calls=%fused_computation.7 | convolution fusion | flops 809501184 | bytes 16777280 | tf_op jit(solution)/shard_map/dot_general | solution.py:24
  184.9 55.7 %convolution_bitcast_fusion = f32[32,64,32,64]{3,1,2,0:T(8,128)} fusion(bf16[32,64,8,256,1]{3,0,1,2,4:T(8,128)(2,1)} %bitcast.38, bf16[32,64,8,256]{3,0,1,2:T(8,128)(2,1)} %bitcast.39), kind=kOutput, calls=%fused_computation.3 | convolution fusion | flops 17179869184 | bytes 33554432 | tf_op jit(solution)/shard_map/dot_general | solution.py:41
  240.6 18.2 %gather_fusion.1 = f32[512,64,64]{2,1,0:T(8,128)} fusion(f32[32,64,32,64]{3,1,2,0:T(8,128)} %convolution_bitcast_fusion, s32[512]{0:T(512)S(1)} %fusion.10), kind=kCustom, calls=%fused_computation.1 | custom fusion | bytes 16781312 | tf_op jit(solution)/shard_map/gather | solution.py:43
  258.8 12.7 %copy.23 = f32[512,64,64]{0,2,1:T(8,128)} copy(f32[512,64,64]{2,1,0:T(8,128)} %gather_fusion.1) | data formatting | bytes 16777216 | tf_op jit(solution)/shard_map/gather | solution.py:43
  271.6 0.0 all-reduce.4.cloned.1.call-update
  271.6 161.2 %all-reduce.4.cloned.1.call-done = f32[512,4096]{0,1:T(8,128)} async-done(((f32[512,4096]{0,1:T(8,128)}), f32[512,4096]{0,1:T(8,128)}) %all-reduce.4.cloned.1.call-update) | async-done | bytes 8388624
  432.8 2.2 constant_dynamic-slice_fusion
  435.0 1.3 copy.24
  (4 shorter events, 0.0 us)
Async XLA Ops:
  22.9 5.6 %copy-start.3 = (u32[128]{0:T(128)S(1)}, u32[128]{0:T(128)}, u32[]{:S(2)}) copy-start(u32[128]{0:T(128)} %constant.25) | copy-start | bytes 1540
  22.9 6.9 %copy-start.2 = (s32[2]{0:T(128)S(1)}, s32[2]{0:T(128)}, u32[]{:S(2)}) copy-start(s32[2]{0:T(128)} %param.9) | copy-start | bytes 28
  22.9 103.1 %copy-start = (s32[512]{0:T(512)S(1)}, s32[512]{0:T(512)}, u32[]{:S(2)}) copy-start(s32[512]{0:T(512)} %param.14) | copy-start | bytes 6148
  22.9 103.1 %copy-start.1 = (s32[512]{0:T(512)S(1)}, s32[512]{0:T(512)}, u32[]{:S(2)}) copy-start(s32[512]{0:T(512)} %param.15) | copy-start | bytes 6148
  22.9 103.1 %all-to-all-start = ((f32[2,64,16384]{2,0,1:T(2,128)}), f32[2,64,16384]{2,0,1:T(2,128)}, u32[]{:S(2)}, u32[]{:S(2)}) async-start(f32[2,64,16384]{2,0,1:T(2,128)} %copy.18), calls=%async_computation | async-start | bytes 16777216 | tf_op jit(solution)/shard_map/all_to_all | solution.py:36
  28.5 404.4 %all-reduce.4.cloned.1.call-start = ((), (), s32[]{:S(2)}) async-start(), calls=%async_computation.1 | async-start | bytes 16777216
Sparse Core Ops, SparseCore 0:
  271.7 161.0 all-reduce.3
where the time goes:
time: 445 us; the launch traced here: 443 us
  waiting for transfers between devices  161 us (36%)
  blocking collectives  95.9 us (22%)
  local copies, waits for them, and re-layouts  93.3 us (21%)
  matrix products  71.6 us (16%)
  between operations  14.8 us (3%)
  starting transfers between devices  5.58 us (1%)
    unnamed x2, waiting for transfers between devices  161 us
    unnamed x1, blocking collectives  95.9 us
    dot_general x1, matrix products, on_device(): jnp.dot(halves, halves.T, preferred_element_type=jnp.float32)  55.7 us
    dot_general x2, local copies, waits for them, and re-layouts, tile_sums(): jnp.dot(onehot, products.reshape(products.shape[0], -1), precision=lax.Pr...  31 us
    gather x2, local copies, waits for them, and re-layouts, on_device(): blocks = gram[pair_mu, :, pair_nu, :]  30.9 us
    unnamed x14, local copies, waits for them, and re-layouts  11.9 us
    dot_general x1, matrix products, tile_sums(): jnp.dot(onehot, products.reshape(products.shape[0], -1), precision=lax.Pr...  11.7 us
  transfers between devices with their start and end apart: 2, of which 1 were waited for; matrix products, arithmetic and copies ran while one was open for 0% of the time, Pallas kernels for 0%

commit v1 on v0

v1 whole, which is shorter than its diff:
```python
import functools

import jax
import jax.numpy as jnp
from jax import lax
from jax.experimental import pallas as pl
from jax.experimental.pallas import tpu as pltpu
from jax.sharding import PartitionSpec as P

TILE = 64
AUX_DEV = 256
OCC = 64
SUP = 16
WT = 32
N_ORB = 8
SLOTS = 16
QS = 4
COLS = AUX_DEV * TILE // (QS * N_ORB)
ROWS = COLS // 128 * OCC
MESH = pl.DeviceIdType.MESH
VMEM = pl.BlockSpec(memory_space=pltpu.VMEM)
SMEM = pl.BlockSpec(memory_space=pltpu.SMEM)
LIMIT = 60 * 1024 * 1024

OFFSETS = ((2, 0), (2, 1), (1, 0), (3, 0), (1, 1), (3, 1), (0, 1))


def gram_kernel(
    nu_ref,
    live_ref,
    support_ref,
    coeffs_ref,
    mu_ref,
    ints_hbm,
    g_ref,
    mus_ref,
    ints,
    sbuf,
    rbuf,
    gsend,
    gpeer,
    in_sem,
    send_sem,
    recv_sem,
    mu_send,
    mu_recv,
    g_send,
    g_recv,
):
    aux = lax.axis_index("aux")
    me = lax.axis_index("orb")
    z, core = me // 2, lax.rem(me, 2)
    others = [lax.rem(z + dz, 4) * 2 + lax.rem(core + dc, 2) for dz, dc in OFFSETS]
    peer = others[-1]

    loads = []
    for q in range(QS):
        load = pltpu.make_async_copy(
            ints_hbm.at[:, :, pl.ds(q * COLS * N_ORB, COLS * N_ORB)], ints.at[q], in_sem.at[q]
        )
        load.start()
        loads.append(load)

    barrier = pltpu.get_barrier_semaphore()
    for other in others:
        pl.semaphore_signal(barrier, inc=1, device_id=(aux, other), device_id_type=MESH)

    lane = lax.broadcasted_iota(jnp.int32, (OCC, 128), 1)
    low = lane < TILE
    support = support_ref[...]
    halves = []
    for s in range(2):
        acc = jnp.zeros((OCC, 128), jnp.float32)
        for jj in range(SUP // 2):
            tile = jnp.where(low, support[:, 2 * jj : 2 * jj + 1], support[:, 2 * jj + 1 : 2 * jj + 2])
            block = coeffs_ref[:, jj * 128 : (jj + 1) * 128].astype(jnp.float32)
            acc = acc + jnp.where(tile == nu_ref[s], block, 0.0)
        acc = acc + pltpu.roll(acc, 64, 1)
        live = jnp.where(s < live_ref[0], 1.0, 0.0)
        keep = low if s == 0 else jnp.logical_not(low)
        halves.append(jnp.where(keep, acc * live, 0.0))
    coef = jnp.concatenate(halves, axis=0).astype(jnp.bfloat16)

    pl.semaphore_wait(barrier, len(others))
    mu_copies = []
    for t, other in enumerate(others):
        copy = pltpu.make_async_remote_copy(
            src_ref=mu_ref,
            dst_ref=mus_ref.at[me],
            send_sem=mu_send.at[t],
            recv_sem=mu_recv.at[me],
            device_id=(aux, other),
            device_id_type=MESH,
        )
        copy.start()
        mu_copies.append(copy)
    mus_ref[me] = mu_ref[...]

    def products(q, dest, store):
        block = ints[q, :, :, pl.ds(pl.multiple_of(dest * COLS, COLS), COLS)].reshape(2 * TILE, COLS)
        res = jnp.dot(coef, block, preferred_element_type=jnp.float32)
        for p in range(COLS // 128):
            a = res[:OCC, p * 128 : (p + 1) * 128]
            b = res[OCC:, p * 128 : (p + 1) * 128]
            even = jnp.where(low, a, pltpu.roll(b, 64, 1))
            odd = jnp.where(low, pltpu.roll(a, 64, 1), b)
            store(p * OCC, even.astype(jnp.bfloat16))
            store(ROWS + p * OCC, odd.astype(jnp.bfloat16))

    def data_copy(q, t):
        return pltpu.make_async_remote_copy(
            src_ref=sbuf.at[q, t],
            dst_ref=rbuf.at[q, me],
            send_sem=send_sem.at[q, t],
            recv_sem=recv_sem.at[q, me],
            device_id=(aux, others[t]),
            device_id_type=MESH,
        )

    for q in range(QS):
        loads[q].wait()
    g_ref[...] = jnp.zeros_like(g_ref)

    @pl.loop(0, QS)
    def _(q):
        for t, other in enumerate(others):

            def to_send(row, value):
                sbuf[q, t, row : row + OCC, :] = value

            products(q, other, to_send)
            data_copy(q, t).start()

        def to_own(row, value):
            rbuf[q, me, row : row + OCC, :] = value

        products(q, me, to_own)

    @pl.loop(0, QS)
    def _(q):
        for other in others:
            pltpu.make_async_remote_copy(
                src_ref=sbuf.at[q, 0],
                dst_ref=rbuf.at[q, other],
                send_sem=send_sem.at[q, 0],
                recv_sem=recv_sem.at[q, other],
                device_id=(aux, other),
                device_id_type=MESH,
            ).wait_recv()

        @pl.loop(0, 4)
        def _(r):
            left = jnp.concatenate([rbuf[q, 2 * r], rbuf[q, 2 * r + 1]], axis=1)
            for c in range(4):
                right = jnp.concatenate([rbuf[q, 2 * c], rbuf[q, 2 * c + 1]], axis=1)
                g_ref[pl.ds(pl.multiple_of(r * 256, 256), 256), c * 256 : (c + 1) * 256] += lax.dot_general(
                    left, right, (((0,), (0,)), ((), ())), preferred_element_type=jnp.float32
                )

    gsend[...] = g_ref[...].astype(jnp.bfloat16)
    swap = pltpu.make_async_remote_copy(
        src_ref=gsend,
        dst_ref=gpeer,
        send_sem=g_send,
        recv_sem=g_recv,
        device_id=(aux, peer),
        device_id_type=MESH,
    )
    swap.start()
    for t, other in enumerate(others):
        mu_copies[t].wait_send()
        pltpu.make_async_remote_copy(
            src_ref=mu_ref,
            dst_ref=mus_ref.at[other],
            send_sem=mu_send.at[t],
            recv_sem=mu_recv.at[other],
            device_id=(aux, other),
            device_id_type=MESH,
        ).wait_recv()

    @pl.loop(0, QS)
    def _(q):
        for t in range(len(others)):
            data_copy(q, t).wait_send()

    swap.wait()
    g_ref[...] += gpeer[...].astype(jnp.float32)


def slab_gram(nu, live, support, coeffs, mu, ints):
    dma = pltpu.SemaphoreType.DMA
    return pl.pallas_call(
        gram_kernel,
        out_shape=(
            jax.ShapeDtypeStruct((SLOTS * TILE, SLOTS * TILE), jnp.float32),
            jax.ShapeDtypeStruct((N_ORB, 8, 128), jnp.int32),
        ),
        in_specs=[SMEM, SMEM, VMEM, VMEM, VMEM, pl.BlockSpec(memory_space=pl.ANY)],
        out_specs=(VMEM, VMEM),
        scratch_shapes=[
            pltpu.VMEM((QS, 2, TILE, COLS * N_ORB), jnp.bfloat16),
            pltpu.VMEM((QS, N_ORB - 1, 2 * ROWS, 128), jnp.bfloat16),
            pltpu.VMEM((QS, N_ORB, 2 * ROWS, 128), jnp.bfloat16),
            pltpu.VMEM((SLOTS * TILE, SLOTS * TILE), jnp.bfloat16),
            pltpu.VMEM((SLOTS * TILE, SLOTS * TILE), jnp.bfloat16),
            dma((QS,)),
            dma((QS, N_ORB - 1)),
            dma((QS, N_ORB)),
            dma((N_ORB - 1,)),
            dma((N_ORB,)),
            dma(()),
            dma(()),
        ],
        compiler_params=pltpu.CompilerParams(
            collective_id=0, has_side_effects=True, vmem_limit_bytes=LIMIT
        ),
        name="slab_gram",
    )(nu, live, support, coeffs, mu, ints)


def pick_kernel(mu_ref, pm_ref, pn_ref, g_in, a_ref, b_ref, g, first):
    core = lax.rem(lax.axis_index("orb"), 2)
    lane = lax.broadcasted_iota(jnp.int32, (TILE, 128), 1)
    low = lane < TILE

    @pl.loop(0, WT)
    def _(w):
        first[w] = SLOTS

    for s in reversed(range(SLOTS)):
        first[mu_ref[s]] = s
    g[...] = g_in[...]

    @pl.loop(1, SLOTS)
    def _(t):
        u = first[mu_ref[t]]

        @pl.when(u < t)
        def _():
            to = pl.ds(pl.multiple_of(u * TILE, TILE), TILE)
            g[to, :] += g[pl.ds(pl.multiple_of(t * TILE, TILE), TILE), :]

    @pl.loop(1, SLOTS)
    def _(t):
        u = first[mu_ref[t]]

        @pl.when(u < t)
        def _():
            shift = lax.rem(t + u, 2) * TILE
            keep = (lane >= TILE) == (lax.rem(u, 2) == 1)

            @pl.loop(0, SLOTS)
            def _(r):
                rows = pl.ds(pl.multiple_of(r * TILE, TILE), TILE)
                source = g[rows, pl.ds(pl.multiple_of(t // 2 * 128, 128), 128)]
                to = pl.ds(pl.multiple_of(u // 2 * 128, 128), 128)
                g[rows, to] += jnp.where(keep, pltpu.roll(source, shift, 1), 0.0)

    def tile_of(k, half):
        u, v = first[pm_ref[k]], first[pn_ref[k]]
        there = jnp.logical_and(u < SLOTS, v < SLOTS)
        u, v = jnp.minimum(u, SLOTS - 1), jnp.minimum(v, SLOTS - 1)
        rows = pl.ds(pl.multiple_of(u * TILE, TILE), TILE)
        tile = g[rows, pl.ds(pl.multiple_of(v // 2 * 128, 128), 128)]
        shift = lax.rem(v + half, 2) * TILE
        return pltpu.roll(tile, shift, 1) * jnp.where(there, 1.0, 0.0)

    @pl.loop(0, 64)
    def _(b):
        y, x, zz = b // 16, lax.rem(b // 4, 4), lax.rem(b, 4)
        k = b // 4 * 32 + zz * 8 + core * 4
        a_ref[x, y, zz] = jnp.where(low, tile_of(k, 0), tile_of(k + 1, 1)).astype(jnp.bfloat16)
        b_ref[y, x, zz] = jnp.where(low, tile_of(k + 2, 0), tile_of(k + 3, 1)).astype(jnp.bfloat16)


def pick(mus, pair_mu, pair_nu, gram):
    half = jax.ShapeDtypeStruct((4, 4, 4, TILE, 128), jnp.bfloat16)
    return pl.pallas_call(
        pick_kernel,
        out_shape=(half, half),
        in_specs=[SMEM, SMEM, SMEM, VMEM],
        out_specs=(VMEM, VMEM),
        scratch_shapes=[
            pltpu.VMEM((SLOTS * TILE, SLOTS * TILE), jnp.float32),
            pltpu.SMEM((WT,), jnp.int32),
        ],
        compiler_params=pltpu.CompilerParams(vmem_limit_bytes=LIMIT),
        name="pick",
    )(mus, pair_mu, pair_nu, gram)


def reduce_kernel(
    a_ref, b_ref, out_ref, ra1, rb1, sa, sb, ra2, rb2, sz, rz, send_sem, recv_sem
):
    aux, orb = lax.axis_index("aux"), lax.axis_index("orb")
    y, x, z, core = aux // 4, lax.rem(aux, 4), orb // 2, lax.rem(orb, 2)

    def along(axis, step):
        if axis == "x":
            return (y * 4 + lax.rem(x + step, 4), orb)
        if axis == "y":
            return (lax.rem(y + step, 4) * 4 + x, orb)
        return (aux, lax.rem(z + step, 4) * 2 + core)

    place = {"x": x, "y": y, "z": z}
    barrier = pltpu.get_barrier_semaphore()
    for axis in "xyz":
        for step in (1, 2, 3):
            pl.semaphore_signal(barrier, inc=1, device_id=along(axis, step), device_id_type=MESH)
    pl.semaphore_wait(barrier, 9)

    def send(stage, axis, source, landing):
        copies = []
        here = place[axis]
        for step in (2, 1, 3):
            there = lax.rem(here + step, 4)
            copy = pltpu.make_async_remote_copy(
                src_ref=source.at[there],
                dst_ref=landing.at[4 - step - 1],
                send_sem=send_sem.at[stage, step - 1],
                recv_sem=recv_sem.at[stage, 4 - step - 1],
                device_id=along(axis, step),
                device_id_type=MESH,
            )
            copy.start()
            copies.append(copy)
        return copies

    def total(axis, source, landing, rest):
        own = source[(place[axis],) + rest].astype(jnp.float32)
        for i in range(3):
            own = own + landing[(i,) + rest].astype(jnp.float32)
        return own

    copies_a = send(0, "x", a_ref, ra1)
    copies_b = send(1, "y", b_ref, rb1)
    for copy in copies_a:
        copy.wait_recv()
    for i in range(4):
        sa[i] = total("x", a_ref, ra1, (i,)).astype(jnp.bfloat16)
    more_a = send(2, "y", sa, ra2)
    for copy in copies_b:
        copy.wait_recv()
    for i in range(4):
        sb[i] = total("y", b_ref, rb1, (i,)).astype(jnp.bfloat16)
    more_b = send(3, "x", sb, rb2)
    for copy in more_a:
        copy.wait_recv()
    for i in range(4):
        sz[i, 0] = total("y", sa, ra2, (i,)).astype(jnp.bfloat16)
    for copy in more_b:
        copy.wait_recv()
    for i in range(4):
        sz[i, 1] = total("x", sb, rb2, (i,)).astype(jnp.bfloat16)
    last = send(4, "z", sz, rz)
    for copy in last:
        copy.wait_recv()
    out_ref[...] = total("z", sz, rz, ())
    for copy in copies_a + copies_b + more_a + more_b + last:
        copy.wait_send()


def reduce_pairs(a, b):
    dma = pltpu.SemaphoreType.DMA
    bf16 = jnp.bfloat16
    return pl.pallas_call(
        reduce_kernel,
        out_shape=jax.ShapeDtypeStruct((2, TILE, 128), jnp.float32),
        in_specs=[VMEM, VMEM],
        out_specs=VMEM,
        scratch_shapes=[
            pltpu.VMEM((3, 4, 4, TILE, 128), bf16),
            pltpu.VMEM((3, 4, 4, TILE, 128), bf16),
            pltpu.VMEM((4, 4, TILE, 128), bf16),
            pltpu.VMEM((4, 4, TILE, 128), bf16),
            pltpu.VMEM((3, 4, TILE, 128), bf16),
            pltpu.VMEM((3, 4, TILE, 128), bf16),
            pltpu.VMEM((4, 2, TILE, 128), bf16),
            pltpu.VMEM((3, 2, TILE, 128), bf16),
            dma((5, 3)),
            dma((5, 3)),
        ],
        compiler_params=pltpu.CompilerParams(
            collective_id=1, has_side_effects=True, vmem_limit_bytes=LIMIT
        ),
        name="reduce_pairs",
    )(a, b)


def on_device(integrals, tile_mu, tile_nu, live_count, support, coeffs, pair_mu, pair_nu):
    mu = jnp.broadcast_to(tile_mu[:, None], (2, 128))
    mu = jnp.concatenate([mu] * 4, axis=0)
    gram, mus = slab_gram(tile_nu, live_count, support, coeffs, mu, integrals)
    mus = mus[:, :2, 0].reshape(SLOTS)
    a, b = pick(mus, pair_mu, pair_nu, gram)
    out = reduce_pairs(a, b)
    return out.reshape(2, TILE, 2, TILE).transpose(0, 2, 1, 3).reshape(4, TILE * TILE)


def solution(mesh):
    return jax.shard_map(
        on_device,
        mesh=mesh,
        in_specs=(
            P(("aux", "orb"), None, None),
            P(("aux", "orb")),
            P(("aux", "orb")),
            P(("aux", "orb")),
            P(),
            P(),
            P(),
            P(),
        ),
        out_specs=P(("aux", "orb"), None),
        check_vma=False,
    )
```

time: 445 us -> 118 us (0.27)
  waiting for transfers between devices: 161 us -> 0 us
  Pallas kernels: 0 us -> 110 us
  blocking collectives: 95.9 us -> 0 us
  local copies, waits for them, and re-layouts: 93.3 us -> 5.4 us
  matrix products: 71.6 us -> 0 us
  between operations: 14.8 us -> 0.69 us
  starting transfers between devices: 5.58 us -> 0 us
    unnamed x2 -> x0, waiting for transfers between devices: 161 us -> none
    pallas_call x0 -> x3, Pallas kernels: none -> 110 us  [the longest x1 62 us: slab_gram(): pl.pallas_call(gram_kernel, out_shape=(jax.ShapeDtypeStruct((SLOTS * TILE...]
    unnamed x1 -> x0, blocking collectives: 95.9 us -> none
    dot_general x4 -> x0, matrix products: 71.6 us -> none  [the longest x1 55.7 us: on_device(): jnp.dot(halves, halves.T, preferred_element_type=jnp.float32)]
    gather x3 -> x0, local copies, waits for them, and re-layouts: 31.5 us -> none  [the longest x2 30.9 us: on_device(): blocks = gram[pair_mu, :, pair_nu, :]]
    dot_general x2 -> x0, local copies, waits for them, and re-layouts: 31 us -> none  [tile_sums(): jnp.dot(onehot, products.reshape(products.shape[0], -1), precision=lax.Pr...]
    unnamed x14 -> x1, local copies, waits for them, and re-layouts: 11.9 us -> 1.39 us
    all_to_all x1 -> x0, local copies, waits for them, and re-layouts: 8.13 us -> none  [on_device(): lax.all_to_all(products, 'orb', split_axis=1, concat_axis=0, tiled=True)]
  transfers between devices with their start and end apart: 2 -> 0, of which waited for: 1 -> 0; matrix products, arithmetic and copies ran while one was open for 0% -> 0% of each run, Pallas kernels for 0% -> 0%
where the time goes in v1:
time: 118 us; the launch traced here: 117 us
  Pallas kernels  110 us (93%)
  local copies, waits for them, and re-layouts  5.4 us (5%)
    pallas_call x1, Pallas kernels, slab_gram(): pl.pallas_call(gram_kernel, out_shape=(jax.ShapeDtypeStruct((SLOTS * TILE...  62 us
    pallas_call x1, Pallas kernels, reduce_pairs(): pl.pallas_call(reduce_kernel, out_shape=jax.ShapeDtypeStruct((2, TILE, 12...  33.3 us
    pallas_call x1, Pallas kernels, pick(): pl.pallas_call(pick_kernel, out_shape=(half, half), in_specs=[SMEM, SMEM,...  15 us

profile of v1, /device:TPU:0, one launch (start us, length us, event | category | flops | bytes accessed | tf_op | source)
XLA Modules:
  0.0 117.0 jit_solution(17454399326052113998)
XLA Ops:
  0.7 0.7 broadcast_in_dim.2
  1.4 0.6 pad_add_fusion.mu_ref
  2.0 1.4 %copy.11.support_ref = s32[64,16]{1,0:T(8,128)} copy(s32[64,16]{0,1:T(8,128)} %param.12) | data formatting | bytes 8192 | tf_op args[4]
  3.4 62.0 %slab_gram.1 = (f32[1024,1024]{1,0:T(8,128)}, s32[8,8,128]{2,1,0:T(8,128)}) custom-call(s32[2]{0:T(128)} %nu_ref.1, s32[1]{0:T(128)S(6)} %copy.13.live_ref, s32[64,16]{1,0:T(8,128)} %copy.11.support_ref, bf16[64,1024]{1,0:T(8,128)(2,1)} %coeffs_ref.1, s32[8,128]{1,0:T(8,128)} %pad_add_fusion.mu_ref, bf16[2,64,16384]{2,1,0:T(8,128)(2,1)} %ints_hbm.1), custom_call_target="tpu_custom_call" | custom-call | tf_op jit(solution)/shard_map/slab_gram/pallas_call | solution.py:192
  65.3 1.0 slice_reduce_fusion
  66.3 0.6 reshape_squeeze.3.mu_ref
  66.9 15.0 %pick.1 = (bf16[4,4,4,64,128]{4,3,2,1,0:T(8,128)(2,1)}, bf16[4,4,4,64,128]{4,3,2,1,0:T(8,128)(2,1)}) custom-call(s32[16]{0:T(128)} %reshape_squeeze.3.mu_ref, s32[512]{0:T(512)} %pm_ref.1, s32[512]{0:T(512)} %pn_ref.1, f32[1024,1024]{1,0:T(8,128)} %get-tuple-element.10.g_in), custom_call_target="tpu_custom_call" | custom-call | tf_op jit(solution)/shard_map/pick/pallas_call | solution.py:278
  82.0 33.3 %reduce_pairs.1 = f32[2,64,128]{2,1,0:T(8,128)} custom-call(bf16[4,4,4,64,128]{4,3,2,1,0:T(8,128)(2,1)} %get-tuple-element.11.a_ref, bf16[4,4,4,64,128]{4,3,2,1,0:T(8,128)(2,1)} %get-tuple-element.12.b_ref), custom_call_target="tpu_custom_call" | custom-call | tf_op jit(solution)/shard_map/reduce_pairs/pallas_call | solution.py:366
  115.3 1.0 reshape.7
  116.3 0.7 reshape.8
  (1 shorter events, 0.0 us)

commit v2 on v1

v2 whole, which is shorter than its diff:
```python
import functools

import jax
import jax.numpy as jnp
from jax import lax
from jax.experimental import pallas as pl
from jax.experimental.pallas import tpu as pltpu
from jax.sharding import PartitionSpec as P

TILE = 64
AUX_DEV = 256
OCC = 64
SUP = 16
WT = 32
N_ORB = 8
POOL = 96
SLOTS = 16
QS = 4
COLS = AUX_DEV * TILE // (QS * N_ORB)
ROWS = COLS // 128 * OCC
MESH = pl.DeviceIdType.MESH
VMEM = pl.BlockSpec(memory_space=pltpu.VMEM)
SMEM = pl.BlockSpec(memory_space=pltpu.SMEM)
LIMIT = 60 * 1024 * 1024

OFFSETS = ((2, 0), (2, 1), (1, 0), (3, 0), (1, 1), (3, 1), (0, 1))


def gram_kernel(
    pool,
    mu_ref,
    nu_ref,
    live_ref,
    support_ref,
    coeffs_ref,
    pm_ref,
    pn_ref,
    ints_hbm,
    g_ref,
    where_ref,
    over_ref,
    ints,
    sbuf,
    rbuf,
    xbuf,
    tiles,
    unpack,
    acc,
    gsend,
    gpeer,
    mine,
    mus,
    in_sem,
    send_sem,
    recv_sem,
    mu_send,
    mu_recv,
    g_send,
    g_recv,
):
    aux = lax.axis_index("aux")
    me = lax.axis_index("orb")
    z, core = me // 2, lax.rem(me, 2)
    others = [lax.rem(z + dz, 4) * 2 + lax.rem(core + dc, 2) for dz, dc in OFFSETS]
    peer = others[-1]

    def load(q):
        return pltpu.make_async_copy(
            ints_hbm.at[:, :, pl.ds(pl.multiple_of(q * COLS * N_ORB, COLS * N_ORB), COLS * N_ORB)],
            ints.at[q],
            in_sem.at[q],
        )

    barrier = pltpu.get_barrier_semaphore()
    for other in others:
        pl.semaphore_signal(barrier, inc=1, device_id=(aux, other), device_id_type=MESH)
    for q in range(QS):
        load(q).start()

    lane = lax.broadcasted_iota(jnp.int32, (OCC, 128), 1)
    low = lane < TILE
    one = (
        lax.broadcasted_iota(jnp.int32, (SUP, SUP), 0) == lax.broadcasted_iota(jnp.int32, (SUP, SUP), 1)
    ).astype(jnp.float32)
    support = lax.dot_general(
        support_ref[...].astype(jnp.float32), one, (((0,), (0,)), ((), ())), preferred_element_type=jnp.float32
    )
    halves = []
    for s in range(2):
        total = jnp.zeros((OCC, 128), jnp.float32)
        nu = nu_ref[s].astype(jnp.float32)
        for jj in range(SUP // 2):
            tile = jnp.where(low, support[:, 2 * jj : 2 * jj + 1], support[:, 2 * jj + 1 : 2 * jj + 2])
            block = coeffs_ref[:, jj * 128 : (jj + 1) * 128].astype(jnp.float32)
            total = total + jnp.where(tile == nu, block, 0.0)
        total = total + pltpu.roll(total, 64, 1)
        live = jnp.where(s < live_ref[0], 1.0, 0.0)
        keep = low if s == 0 else jnp.logical_not(low)
        halves.append(jnp.where(keep, total * live, 0.0))
    coef = jnp.concatenate(halves, axis=0).astype(jnp.bfloat16)

    slot = lax.rem(lax.broadcasted_iota(jnp.int32, (8, 128), 0), 2)
    mine[0] = jnp.where(slot < live_ref[0], jnp.where(slot == 0, mu_ref[0], mu_ref[1]), -1)
    mine[1] = jnp.where(slot < live_ref[0], jnp.where(slot == 0, nu_ref[0], nu_ref[1]), -1)

    for j in range(SUP):
        tiles[j] = jnp.broadcast_to(support[:, j : j + 1], (OCC, 128))
    square = (2 * OCC, 2 * OCC)
    to, at = lax.broadcasted_iota(jnp.int32, square, 0), lax.broadcasted_iota(jnp.int32, square, 1)
    before = jnp.where(at < to, 1.0, 0.0).astype(jnp.bfloat16)

    def placement(nus):
        used = []
        for s in range(2):
            nu = nus[s : s + 1].astype(jnp.float32)
            count = jnp.zeros((OCC, 128), jnp.float32)
            for j in range(SUP):
                count = count + jnp.where(tiles[j] == nu, 1.0, 0.0)
            used.append(count)
        used = jnp.concatenate(used, axis=0)
        rank = jnp.dot(before, used.astype(jnp.bfloat16), preferred_element_type=jnp.float32)
        last = slice(2 * OCC - 1, 2 * OCC)
        placed = jnp.where(rank == at.astype(jnp.float32), used, 0.0)
        return placed.astype(jnp.bfloat16), rank[last] + used[last]

    own, _ = placement(mine[1])
    packed = lax.dot_general(own, coef, (((0,), (0,)), ((), ())), preferred_element_type=jnp.float32)
    packed = packed[:pool].astype(jnp.bfloat16)

    def mu_copy(t, device):
        return pltpu.make_async_remote_copy(
            src_ref=mine,
            dst_ref=mus.at[device],
            send_sem=mu_send.at[t],
            recv_sem=mu_recv.at[device],
            device_id=(aux, others[t]),
            device_id_type=MESH,
        )

    def data_copy(q, t, device):
        return pltpu.make_async_remote_copy(
            src_ref=sbuf.at[q, t],
            dst_ref=rbuf.at[q, device],
            send_sem=send_sem.at[q, t],
            recv_sem=recv_sem.at[q, device],
            device_id=(aux, others[t]),
            device_id_type=MESH,
        )

    def swap(r):
        rows = pl.ds(r * 256, 256)
        return pltpu.make_async_remote_copy(
            src_ref=gsend.at[rows],
            dst_ref=gpeer.at[rows],
            send_sem=g_send.at[r],
            recv_sem=g_recv.at[r],
            device_id=(aux, peer),
            device_id_type=MESH,
        )

    def products(q, dest, store):
        block = ints[q, :, :, pl.ds(pl.multiple_of(dest * COLS, COLS), COLS)].reshape(2 * TILE, COLS)
        res = jnp.dot(packed, block, preferred_element_type=jnp.float32).astype(jnp.bfloat16)
        for p in range(COLS // 128):
            store(p * pool, res[:, p * 128 : (p + 1) * 128])

    pl.semaphore_wait(barrier, len(others))
    for t in range(len(others)):
        mu_copy(t, me).start()

    @pl.loop(0, QS)
    def _(q):
        load(q).wait()
        for t, other in enumerate(others):

            def to_send(row, value):
                sbuf[q, t, row : row + pool, :] = value

            products(q, other, to_send)
            data_copy(q, t, me).start()

        def to_own(row, value):
            rbuf[q, me, row : row + pool, :] = value

        products(q, me, to_own)

    mus[me] = mine[...]
    for t, other in enumerate(others):
        mu_copy(t, other).wait_recv()
    over_ref[...] = jnp.zeros_like(over_ref)

    @pl.loop(0, N_ORB)
    def _(source):
        placed, rows = placement(mus[source, 1])
        unpack[source] = placed
        over_ref[...] = jnp.maximum(over_ref[...], jnp.where(rows > pool, 1.0, 0.0))

    table = mus[:, 0].reshape(N_ORB * 8, 128)[:, :1]
    count = pm_ref.shape[1]
    k = lax.broadcasted_iota(jnp.int32, (N_ORB * 8, count), 1)
    here = lax.rem(k // 4, 2) == core
    rows = jnp.where(table == pm_ref[...], 1.0, 0.0).astype(jnp.bfloat16)
    cols = jnp.logical_and(table == pn_ref[...], here)

    def pairs(value):
        return lax.dot_general(
            rows,
            jnp.where(cols, value.astype(jnp.float32), 0.0).astype(jnp.bfloat16),
            (((1,), (1,)), ((), ())),
            preferred_element_type=jnp.float32,
        )

    found = pairs(k // 32) * 32.0 + pairs(lax.rem(k, 32) + 1) - 1.0
    where_ref[...] = found.astype(jnp.int32)

    acc[...] = jnp.zeros_like(acc)

    def spread(q, source):
        data = rbuf[q, source]
        data = jnp.concatenate([data[p * pool : (p + 1) * pool] for p in range(COLS // 128)], axis=1)
        res = jnp.dot(unpack[source][:, :pool], data, preferred_element_type=jnp.float32)
        for p in range(COLS // 128):
            a = res[:OCC, p * 128 : (p + 1) * 128]
            b = res[OCC:, p * 128 : (p + 1) * 128]
            even = jnp.where(low, a, pltpu.roll(b, 64, 1))
            odd = jnp.where(low, pltpu.roll(a, 64, 1), b)
            xbuf[source, p * OCC : (p + 1) * OCC] = even.astype(jnp.bfloat16)
            xbuf[source, ROWS + p * OCC : ROWS + (p + 1) * OCC] = odd.astype(jnp.bfloat16)

    def gram(r):
        left = jnp.concatenate([xbuf[2 * r], xbuf[2 * r + 1]], axis=1)
        for c in range(4):
            right = jnp.concatenate([xbuf[2 * c], xbuf[2 * c + 1]], axis=1)
            acc[r, :, c * 256 : (c + 1) * 256] += lax.dot_general(
                left, right, (((0,), (0,)), ((), ())), preferred_element_type=jnp.float32
            )

    @pl.loop(0, QS)
    def _(q):
        spread(q, me)
        for t in reversed(range(len(others))):
            data_copy(q, t, others[t]).wait_recv()
            spread(q, others[t])

        @pl.when(q < QS - 1)
        def _():
            @pl.loop(0, 4)
            def _(r):
                gram(r)

    for r in range(4):
        gram(r)
        gsend[r * 256 : (r + 1) * 256] = acc[r].astype(jnp.bfloat16)
        swap(r).start()
    for r in range(4):
        swap(r).wait_recv()
        rows = slice(r * 256, (r + 1) * 256)
        g_ref[rows] = (acc[r] + gpeer[rows].astype(jnp.float32)).astype(jnp.bfloat16)

    for r in range(4):
        swap(r).wait_send()
    for t in range(len(others)):
        mu_copy(t, me).wait_send()

    @pl.loop(0, QS)
    def _(q):
        for t in range(len(others)):
            data_copy(q, t, me).wait_send()


def slab_gram(pool, identity, mu, nu, live, support, coeffs, pair_mu, pair_nu, ints):
    dma = pltpu.SemaphoreType.DMA
    size = SLOTS * TILE
    return pl.pallas_call(
        functools.partial(gram_kernel, pool),
        out_shape=(
            jax.ShapeDtypeStruct((size, size), jnp.bfloat16),
            jax.ShapeDtypeStruct((N_ORB * 8, N_ORB * 8), jnp.int32),
            jax.ShapeDtypeStruct((8, 128), jnp.float32),
        ),
        in_specs=[SMEM] * 3 + [VMEM] * 4 + [pl.BlockSpec(memory_space=pl.ANY)],
        out_specs=(VMEM, VMEM, VMEM),
        scratch_shapes=[
            pltpu.VMEM((QS, 2, TILE, COLS * N_ORB), jnp.bfloat16),
            pltpu.VMEM((QS, N_ORB - 1, COLS // 128 * pool, 128), jnp.bfloat16),
            pltpu.VMEM((QS, N_ORB, COLS // 128 * pool, 128), jnp.bfloat16),
            pltpu.VMEM((N_ORB, 2 * ROWS, 128), jnp.bfloat16),
            pltpu.VMEM((SUP, OCC, 128), jnp.float32),
            pltpu.VMEM((N_ORB, 2 * OCC, 2 * OCC), jnp.bfloat16),
            pltpu.VMEM((4, size // 4, size), jnp.float32),
            pltpu.VMEM((size, size), jnp.bfloat16),
            pltpu.VMEM((size, size), jnp.bfloat16),
            pltpu.VMEM((2, 8, 128), jnp.int32),
            pltpu.VMEM((N_ORB, 2, 8, 128), jnp.int32),
            dma((QS,)),
            dma((QS, N_ORB - 1)),
            dma((QS, N_ORB)),
            dma((N_ORB - 1,)),
            dma((N_ORB,)),
            dma((4,)),
            dma((4,)),
        ],
        compiler_params=pltpu.CompilerParams(
            collective_id=identity, has_side_effects=True, vmem_limit_bytes=LIMIT
        ),
        name="slab_gram",
    )(mu, nu, live, support, coeffs, pair_mu, pair_nu, ints)


def pick_kernel(where_ref, g_ref, e_ref):
    lane = lax.broadcasted_iota(jnp.int32, (TILE, 128), 1)
    high = jnp.where(lane < TILE, 0, 1)
    e_ref[...] = jnp.zeros_like(e_ref)

    @pl.loop(0, SLOTS)
    def _(s):
        rows = pl.ds(pl.multiple_of(s * TILE, TILE), TILE)
        for t in range(SLOTS):
            k = where_ref[s // 2 * 8 + lax.rem(s, 2), t // 2 * 8 + t % 2]

            @pl.when(k >= 0)
            def _():
                half, pair, zz = lax.rem(k, 2), lax.rem(k // 2, 2), lax.rem(k // 8, 4)
                x, y = lax.rem(k // 32, 4), k // 128
                slow, fast = jnp.where(pair == 0, x, y), jnp.where(pair == 0, y, x)
                tile = g_ref[rows, t // 2 * 128 : (t // 2 + 1) * 128].astype(jnp.float32)
                tile = jnp.where(half == t % 2, tile, pltpu.roll(tile, 64, 1))
                e_ref[pair, slow, fast, zz] += jnp.where(high == half, tile, 0.0).astype(jnp.bfloat16)


def pick(where, gram):
    return pl.pallas_call(
        pick_kernel,
        out_shape=jax.ShapeDtypeStruct((2, 4, 4, 4, TILE, 128), jnp.bfloat16),
        in_specs=[SMEM, VMEM],
        out_specs=VMEM,
        compiler_params=pltpu.CompilerParams(vmem_limit_bytes=LIMIT),
        name="pick",
    )(where, gram)


def reduce_kernel(
    e_ref, over_ref, out_ref, any_ref, ra1, rb1, sa, sb, ra2, rb2, sz, rz, done, row, overs, send_sem, recv_sem
):
    aux, orb = lax.axis_index("aux"), lax.axis_index("orb")
    y, x, z, core = aux // 4, lax.rem(aux, 4), orb // 2, lax.rem(orb, 2)

    def along(axis, step):
        if axis == "x":
            return (y * 4 + lax.rem(x + step, 4), orb)
        if axis == "y":
            return (lax.rem(y + step, 4) * 4 + x, orb)
        return (aux, lax.rem(z + step, 4) * 2 + core)

    place = {"x": x, "y": y, "z": z}
    barrier = pltpu.get_barrier_semaphore()
    for axis in "xyz":
        for step in (1, 2, 3):
            pl.semaphore_signal(barrier, inc=1, device_id=along(axis, step), device_id_type=MESH)
    pl.semaphore_wait(barrier, 9)

    def send(stage, axis, source, landing):
        copies = []
        here = place[axis]
        for step in (2, 1, 3):
            there = lax.rem(here + step, 4)
            copy = pltpu.make_async_remote_copy(
                src_ref=source.at[there],
                dst_ref=landing.at[4 - step - 1],
                send_sem=send_sem.at[stage, step - 1],
                recv_sem=recv_sem.at[stage, 4 - step - 1],
                device_id=along(axis, step),
                device_id_type=MESH,
            )
            copy.start()
            copies.append(copy)
        return copies

    def total(axis, source, landing, rest):
        own = source[(place[axis],) + rest].astype(jnp.float32)
        for i in range(3):
            own = own + landing[(i,) + rest].astype(jnp.float32)
        return own

    def tell(stage, axis, source):
        copies = []
        for step in (1, 2, 3):
            copy = pltpu.make_async_remote_copy(
                src_ref=source,
                dst_ref=overs.at[stage - 5, 4 - step - 1],
                send_sem=send_sem.at[stage, step - 1],
                recv_sem=recv_sem.at[stage, 4 - step - 1],
                device_id=along(axis, step),
                device_id_type=MESH,
            )
            copy.start()
            copies.append(copy)
        return copies

    a_ref, b_ref = e_ref.at[0], e_ref.at[1]
    tell_x = tell(5, "x", over_ref)
    copies_a = send(0, "x", a_ref, ra1)
    copies_b = send(1, "y", b_ref, rb1)
    for copy in copies_a:
        copy.wait_recv()
    for copy in tell_x:
        copy.wait_recv()
    row[...] = over_ref[...] + overs[0, 0] + overs[0, 1] + overs[0, 2]
    tell_y = tell(6, "y", row)
    for i in range(4):
        sa[i] = total("x", a_ref, ra1, (i,)).astype(jnp.bfloat16)
    more_a = send(2, "y", sa, ra2)
    for copy in copies_b:
        copy.wait_recv()
    for i in range(4):
        sb[i] = total("y", b_ref, rb1, (i,)).astype(jnp.bfloat16)
    more_b = send(3, "x", sb, rb2)
    for copy in more_a:
        copy.wait_recv()
    for i in range(4):
        sz[i, 0] = total("y", sa, ra2, (i,))
    for copy in more_b:
        copy.wait_recv()
    for i in range(4):
        sz[i, 1] = total("x", sb, rb2, (i,))
    last = send(4, "z", sz, rz)
    for copy in last:
        copy.wait_recv()
    lane = lax.broadcasted_iota(jnp.int32, (TILE // 2, 128), 1)
    low = lane < TILE
    for copy in tell_y:
        copy.wait_recv()
    found = jnp.max(row[...] + overs[1, 0] + overs[1, 1] + overs[1, 2])
    any_ref[0] = jnp.where(found > 0.5, 1, 0)
    done[...] = total("z", sz, rz, ())
    for i in range(2):
        even = done[i, pl.ds(0, TILE // 2, stride=2), :]
        odd = done[i, pl.ds(1, TILE // 2, stride=2), :]
        first = jnp.where(low, even, pltpu.roll(odd, 64, 1))
        second = jnp.where(low, pltpu.roll(even, 64, 1), odd)
        for m in range(TILE // 2):
            out_ref[2 * i : 2 * i + 1, m * 128 : (m + 1) * 128] = first[m : m + 1]
            out_ref[2 * i + 1 : 2 * i + 2, m * 128 : (m + 1) * 128] = second[m : m + 1]
    for copy in copies_a + copies_b + more_a + more_b + last + tell_x + tell_y:
        copy.wait_send()


def reduce_pairs(identity, e, over):
    dma = pltpu.SemaphoreType.DMA
    bf16 = jnp.bfloat16
    return pl.pallas_call(
        reduce_kernel,
        out_shape=(
            jax.ShapeDtypeStruct((4, TILE * TILE), jnp.float32),
            jax.ShapeDtypeStruct((1,), jnp.int32),
        ),
        in_specs=[VMEM, VMEM],
        out_specs=(VMEM, SMEM),
        scratch_shapes=[
            pltpu.VMEM((3, 4, 4, TILE, 128), bf16),
            pltpu.VMEM((3, 4, 4, TILE, 128), bf16),
            pltpu.VMEM((4, 4, TILE, 128), bf16),
            pltpu.VMEM((4, 4, TILE, 128), bf16),
            pltpu.VMEM((3, 4, TILE, 128), bf16),
            pltpu.VMEM((3, 4, TILE, 128), bf16),
            pltpu.VMEM((4, 2, TILE, 128), jnp.float32),
            pltpu.VMEM((3, 2, TILE, 128), jnp.float32),
            pltpu.VMEM((2, TILE, 128), jnp.float32),
            pltpu.VMEM((8, 128), jnp.float32),
            pltpu.VMEM((2, 3, 8, 128), jnp.float32),
            dma((7, 3)),
            dma((7, 3)),
        ],
        compiler_params=pltpu.CompilerParams(
            collective_id=identity, has_side_effects=True, vmem_limit_bytes=LIMIT
        ),
        name="reduce_pairs",
    )(e, over)


def on_device(integrals, tile_mu, tile_nu, live_count, support, coeffs, pair_mu, pair_nu):
    args = (tile_mu, tile_nu, live_count, support.T, coeffs, pair_mu[None, :], pair_nu[None, :], integrals)

    def exchange(pool, identity):
        gram, where, over = slab_gram(pool, identity, *args)
        return reduce_pairs(identity + 1, pick(where, gram), over)

    out, over = exchange(POOL, 0)
    return lax.cond(over[0] == 0, lambda: out, lambda: exchange(2 * OCC, 2)[0])


def solution(mesh):
    return jax.shard_map(
        on_device,
        mesh=mesh,
        in_specs=(
            P(("aux", "orb"), None, None),
            P(("aux", "orb")),
            P(("aux", "orb")),
            P(("aux", "orb")),
            P(),
            P(),
            P(),
            P(),
        ),
        out_specs=P(("aux", "orb"), None),
        check_vma=False,
    )
```

time: 118 us -> 93 us (0.79)
  Pallas kernels: 110 us -> 89.7 us
  local copies, waits for them, and re-layouts: 5.4 us -> 0.66 us
    pallas_call x3, Pallas kernels: 110 us -> 89.7 us  [the longest x1 49.6 us: slab_gram(): pl.pallas_call(functools.partial(gram_kernel, pool), out_shape=(jax.Shape...]
    reshape x2 -> x0, local copies, waits for them, and re-layouts: 1.7 us -> none  [on_device(): out.reshape(2, TILE, 2, TILE).transpose(0, 2, 1, 3).reshape(4, TILE * TILE)]
where the time goes in v2:
time: 93 us; the launch traced here: 92 us
  Pallas kernels  89.7 us (96%)
  between operations  1.42 us (2%)
    pallas_call x1, Pallas kernels, slab_gram(): pl.pallas_call(functools.partial(gram_kernel, pool), out_shape=(jax.Shape...  49.6 us
    pallas_call x1, Pallas kernels, reduce_pairs(): pl.pallas_call(reduce_kernel, out_shape=(jax.ShapeDtypeStruct((4, TILE *...  32.1 us
    pallas_call x1, Pallas kernels, pick(): pl.pallas_call(pick_kernel, out_shape=jax.ShapeDtypeStruct((2, 4, 4, 4, T...  7.98 us

profile of v2, /device:TPU:0, one launch (start us, length us, event | category | flops | bytes accessed | tf_op | source)
XLA Modules:
  0.0 92.0 jit_solution(13583114433381636714)
XLA Ops:
  0.7 49.6 %slab_gram.3 = (bf16[1024,1024]{1,0:T(8,128)(2,1)}, s32[64,64]{1,0:T(8,128)}, f32[8,128]{1,0:T(8,128)}) custom-call(s32[2]{0:T(128)} %mu_ref.1, s32[2]{0:T(128)} %nu_ref.1, s32[1]{0:T(128)S(6)} %copy.14.live_ref, s32[16,64]{1,0:T(8,128)} %bitcast.4, bf16[64,1024]{1,0:T(8,128)(2,1)} %coeffs_ref.1, s32[1,512]{1,0:T(1,128)} %bitcast.6, s32[1,512]{1,0:T(1,128)} %bitcast.8, ...), custom_call_target="tpu_custom_call" | custom-call | tf_op jit(solution)/shard_map/slab_gram/pallas_call | solution.py:274
  50.3 8.0 %pick.3.e_ref = bf16[2,4,4,4,64,128]{5,4,3,2,1,0:T(8,128)(2,1)} custom-call(s32[64,64]{1,0:T(8,128)} %get-tuple-element.42.where_ref, bf16[1024,1024]{1,0:T(8,128)(2,1)} %get-tuple-element.43.g_ref), custom_call_target="tpu_custom_call" | custom-call | tf_op jit(solution)/shard_map/pick/pallas_call | solution.py:332
  58.3 0.0 copy-start
  58.3 0.0 copy-start.1
  58.3 0.0 copy-start.2
  58.3 0.0 copy-start.3
  58.3 0.0 copy-start.4
  58.3 0.0 copy-start.5
  58.3 32.1 %reduce_pairs.3 = (f32[4,4096]{1,0:T(4,128)S(1)}, s32[1]{0:T(128)}) custom-call(bf16[2,4,4,4,64,128]{5,4,3,2,1,0:T(8,128)(2,1)} %pick.3.e_ref, f32[8,128]{1,0:T(8,128)} %get-tuple-element.44.over_ref), custom_call_target="tpu_custom_call" | custom-call | tf_op jit(solution)/shard_map/reduce_pairs/pallas_call | solution.py:451
  91.1 0.0 copy-done
  91.1 0.0 copy-done.1
  91.1 0.0 copy-done.2
  91.1 0.0 copy-done.3
  91.1 0.0 copy-done.4
  91.1 0.0 copy-done.5
  91.1 0.2 conditional.1
  91.3 0.6 copy.15
Async XLA Ops:
  58.3 32.8 %copy-start = (bf16[64,1024]{1,0:T(8,128)(2,1)S(1)}, bf16[64,1024]{1,0:T(8,128)(2,1)}, u32[]{:S(2)}) copy-start(bf16[64,1024]{1,0:T(8,128)(2,1)} %coeffs_ref.1) | copy-start | bytes 393220
  58.3 32.8 %copy-start.1 = (s32[64,16]{0,1:T(8,128)S(1)}, s32[64,16]{0,1:T(8,128)}, u32[]{:S(2)}) copy-start(s32[64,16]{0,1:T(8,128)} %param.14) | copy-start | bytes 12292
  58.3 32.8 %copy-start.2 = (s32[512]{0:T(512)S(1)}, s32[512]{0:T(512)}, u32[]{:S(2)}) copy-start(s32[512]{0:T(512)} %param.16) | copy-start | bytes 6148
  58.3 32.8 %copy-start.3 = (s32[512]{0:T(512)S(1)}, s32[512]{0:T(512)}, u32[]{:S(2)}) copy-start(s32[512]{0:T(512)} %param.17) | copy-start | bytes 6148
  58.3 32.8 %copy-start.4 = (s32[2]{0:T(128)S(1)}, s32[2]{0:T(128)}, u32[]{:S(2)}) copy-start(s32[2]{0:T(128)} %mu_ref.1) | copy-start | bytes 28
  58.3 32.8 %copy-start.5 = (s32[2]{0:T(128)S(1)}, s32[2]{0:T(128)}, u32[]{:S(2)}) copy-start(s32[2]{0:T(128)} %nu_ref.1) | copy-start | bytes 28

commit v3 on v2

v3 whole, which is shorter than its diff:
```python
import functools

import jax
import jax.numpy as jnp
from jax import lax
from jax.experimental import pallas as pl
from jax.experimental.pallas import tpu as pltpu
from jax.sharding import PartitionSpec as P

TILE = 64
AUX_DEV = 256
OCC = 64
SUP = 16
WT = 32
N_ORB = 8
POOL = 96
SLOTS = 16
QS = 4
COLS = AUX_DEV * TILE // (QS * N_ORB)
ROWS = COLS // 128 * OCC
CUT = 48
MESH = pl.DeviceIdType.MESH
VMEM = pl.BlockSpec(memory_space=pltpu.VMEM)
SMEM = pl.BlockSpec(memory_space=pltpu.SMEM)
LIMIT = 60 * 1024 * 1024

OFFSETS = ((2, 0), (2, 1), (1, 0), (3, 0), (1, 1), (3, 1), (0, 1))


STEPS = (2, 1, 3)
BLOCKS = 17 * 16


def exchange_kernel(
    pool,
    mu_ref,
    nu_ref,
    live_ref,
    support_ref,
    coeffs_ref,
    pm_ref,
    pn_ref,
    ints_hbm,
    out_ref,
    any_ref,
    ints,
    sbuf,
    rbuf,
    xbuf,
    tiles,
    unpack,
    merge,
    stack,
    first,
    acc,
    gsend,
    gpeer,
    blocks,
    index,
    index_smem,
    mine,
    mus,
    over,
    row,
    overs,
    done,
    e_a,
    e_b,
    e_c,
    r1_a,
    r1_b,
    r1_c,
    s2_a,
    s2_b,
    s2_c,
    r2_a,
    r2_b,
    r2_c,
    s3_a,
    s3_b,
    s3_c,
    r3_a,
    r3_b,
    r3_c,
    in_sem,
    send_sem,
    recv_sem,
    mu_send,
    mu_recv,
    g_send,
    g_recv,
    index_sem,
    tell_send,
    tell_recv,
    ring_send,
    ring_recv,
):
    aux = lax.axis_index("aux")
    me = lax.axis_index("orb")
    y, x = aux // 4, lax.rem(aux, 4)
    z, core = me // 2, lax.rem(me, 2)
    others = [lax.rem(z + dz, 4) * 2 + lax.rem(core + dc, 2) for dz, dc in OFFSETS]
    peer = others[-1]
    place = {"x": x, "y": y, "z": z}

    def along(axis, step):
        if axis == "x":
            return (y * 4 + lax.rem(x + step, 4), me)
        if axis == "y":
            return (lax.rem(y + step, 4) * 4 + x, me)
        return (aux, lax.rem(z + step, 4) * 2 + core)

    def load(q):
        return pltpu.make_async_copy(
            ints_hbm.at[:, :, pl.ds(pl.multiple_of(q * COLS * N_ORB, COLS * N_ORB), COLS * N_ORB)],
            ints.at[q],
            in_sem.at[q],
        )

    barrier = pltpu.get_barrier_semaphore()
    for other in others:
        pl.semaphore_signal(barrier, inc=1, device_id=(aux, other), device_id_type=MESH)
    for axis in "xy":
        for step in STEPS:
            pl.semaphore_signal(barrier, inc=1, device_id=along(axis, step), device_id_type=MESH)
    for q in range(QS):
        load(q).start()

    lane = lax.broadcasted_iota(jnp.int32, (OCC, 128), 1)
    low = lane < TILE
    one = (
        lax.broadcasted_iota(jnp.int32, (SUP, SUP), 0) == lax.broadcasted_iota(jnp.int32, (SUP, SUP), 1)
    ).astype(jnp.float32)
    support = lax.dot_general(
        support_ref[...].astype(jnp.float32), one, (((0,), (0,)), ((), ())), preferred_element_type=jnp.float32
    )
    halves = []
    for s in range(2):
        total = jnp.zeros((OCC, 128), jnp.float32)
        nu = nu_ref[s].astype(jnp.float32)
        for jj in range(SUP // 2):
            tile = jnp.where(low, support[:, 2 * jj : 2 * jj + 1], support[:, 2 * jj + 1 : 2 * jj + 2])
            block = coeffs_ref[:, jj * 128 : (jj + 1) * 128].astype(jnp.float32)
            total = total + jnp.where(tile == nu, block, 0.0)
        total = total + pltpu.roll(total, 64, 1)
        live = jnp.where(s < live_ref[0], 1.0, 0.0)
        keep = low if s == 0 else jnp.logical_not(low)
        halves.append(jnp.where(keep, total * live, 0.0))
    coef = jnp.concatenate(halves, axis=0).astype(jnp.bfloat16)

    slot = lax.rem(lax.broadcasted_iota(jnp.int32, (8, 128), 0), 2)
    mine[0] = jnp.where(slot < live_ref[0], jnp.where(slot == 0, mu_ref[0], mu_ref[1]), -1)
    mine[1] = jnp.where(slot < live_ref[0], jnp.where(slot == 0, nu_ref[0], nu_ref[1]), -1)

    for j in range(SUP):
        tiles[j] = jnp.broadcast_to(support[:, j : j + 1], (OCC, 128))
    square = (2 * OCC, 2 * OCC)
    to, at = lax.broadcasted_iota(jnp.int32, square, 0), lax.broadcasted_iota(jnp.int32, square, 1)
    before = jnp.where(at < to, 1.0, 0.0).astype(jnp.bfloat16)

    def placement(nus):
        used = []
        for s in range(2):
            nu = nus[s : s + 1].astype(jnp.float32)
            count = jnp.zeros((OCC, 128), jnp.float32)
            for j in range(SUP):
                count = count + jnp.where(tiles[j] == nu, 1.0, 0.0)
            used.append(count)
        used = jnp.concatenate(used, axis=0)
        rank = jnp.dot(before, used.astype(jnp.bfloat16), preferred_element_type=jnp.float32)
        last = slice(2 * OCC - 1, 2 * OCC)
        placed = jnp.where(rank == at.astype(jnp.float32), used, 0.0)
        return placed.astype(jnp.bfloat16), rank[last] + used[last]

    own, _ = placement(mine[1])
    packed = lax.dot_general(own, coef, (((0,), (0,)), ((), ())), preferred_element_type=jnp.float32)
    packed = packed[:pool].astype(jnp.bfloat16)

    def mu_copy(t, device):
        return pltpu.make_async_remote_copy(
            src_ref=mine,
            dst_ref=mus.at[device],
            send_sem=mu_send.at[t],
            recv_sem=mu_recv.at[device],
            device_id=(aux, others[t]),
            device_id_type=MESH,
        )

    def data_copy(q, t, device):
        return pltpu.make_async_remote_copy(
            src_ref=sbuf.at[q, t],
            dst_ref=rbuf.at[q, device],
            send_sem=send_sem.at[q, t],
            recv_sem=recv_sem.at[q, device],
            device_id=(aux, others[t]),
            device_id_type=MESH,
        )

    def swap(r):
        rows = pl.ds(r * 256, 256)
        return pltpu.make_async_remote_copy(
            src_ref=gsend.at[rows],
            dst_ref=gpeer.at[rows],
            send_sem=g_send.at[r],
            recv_sem=g_recv.at[r],
            device_id=(aux, peer),
            device_id_type=MESH,
        )

    def products(q, dest, store):
        block = ints[q, :, :, pl.ds(pl.multiple_of(dest * COLS, COLS), COLS)].reshape(2 * TILE, COLS)
        res = jnp.dot(packed, block, preferred_element_type=jnp.float32).astype(jnp.bfloat16)
        for p in range(COLS // 128):
            store(p * pool, res[:, p * 128 : (p + 1) * 128])

    def tell(stage, axis, source):
        return [
            pltpu.make_async_remote_copy(
                src_ref=source,
                dst_ref=overs.at[stage, 3 - step],
                send_sem=tell_send.at[stage, step - 1],
                recv_sem=tell_recv.at[stage, 3 - step],
                device_id=along(axis, step),
                device_id_type=MESH,
            )
            for step in STEPS
        ]

    pl.semaphore_wait(barrier, len(others) + 6)
    for t in range(len(others)):
        mu_copy(t, me).start()

    @pl.loop(0, QS)
    def _(q):
        load(q).wait()
        for t, other in enumerate(others):

            def to_send(row, value):
                sbuf[q, t, row : row + pool, :] = value

            products(q, other, to_send)
            data_copy(q, t, me).start()

        def to_own(row, value):
            rbuf[q, me, row : row + pool, :] = value

        products(q, me, to_own)

    mus[me] = mine[...]
    for t, other in enumerate(others):
        mu_copy(t, other).wait_recv()
    over[...] = jnp.zeros_like(over)

    @pl.loop(0, N_ORB)
    def _(source):
        placed, rows = placement(mus[source, 1])
        unpack[source] = placed.astype(jnp.float32).T
        over[...] = jnp.maximum(over[...], jnp.where(rows > pool, 1.0, 0.0))

    tell_x = tell(0, "x", over)
    for copy in tell_x:
        copy.start()

    def mu_of(slot):
        return mus[slot // 2, 0, slot % 2 : slot % 2 + 1]

    for s in range(SLOTS):
        is_first = jnp.ones((1, 128), jnp.int32)
        for t in range(s):
            is_first = jnp.where(mu_of(t) == mu_of(s), 0, is_first)
        first[s : s + 1] = jnp.where(mu_of(s) >= 0, is_first, 0)
    low_row = low[:1]
    for pair in range(N_ORB):

        @pl.loop(0, N_ORB)
        def _(source):
            def shares(slot, s):
                same = mus[source, 0, s : s + 1] == mu_of(slot)
                return jnp.where(same, first[slot : slot + 1], 0).astype(jnp.float32)

            kept = jnp.where(low_row, shares(2 * pair, 0), shares(2 * pair + 1, 1))
            turned = jnp.where(low_row, shares(2 * pair, 1), shares(2 * pair + 1, 0))
            placed = unpack[source]
            both = placed * kept + pltpu.roll(placed, 64, 1) * turned
            at_row = pl.ds(pl.multiple_of(source * pool, pool), pool)
            stack[at_row] = both[:pool]

        merge[pair] = stack[...].T.astype(jnp.bfloat16)

    k = lax.broadcasted_iota(jnp.int32, pm_ref.shape, 1)
    u = jnp.full(pm_ref.shape, SLOTS, jnp.int32)
    v = jnp.full(pm_ref.shape, -1, jnp.int32)
    for s in range(SLOTS):
        known = first[s : s + 1, :1] > 0
        tile = mu_of(s)[:, :1]
        u = jnp.where(jnp.logical_and(known, pm_ref[...] == tile), s, u)
        v = jnp.where(jnp.logical_and(known, pn_ref[...] == tile), s, v)
    u = jnp.where(v >= 0, u, SLOTS)
    v = jnp.maximum(v, 0)
    index[...] = (((v + k) & 1) * 8 + (v >> 1)) * 17 + u
    to_smem = pltpu.make_async_copy(index, index_smem, index_sem)
    to_smem.start()
    for c in range(16):
        blocks[c * 17 + 16] = jnp.zeros((TILE, 128), jnp.bfloat16)

    for copy in tell_x:
        copy.wait_recv()
    row[...] = over[...] + overs[0, 0] + overs[0, 1] + overs[0, 2]
    tell_y = tell(1, "y", row)
    for copy in tell_y:
        copy.start()

    acc[...] = jnp.zeros_like(acc)

    def spread(q):
        @pl.loop(0, N_ORB)
        def _(pair):
            data = jnp.concatenate(
                [
                    jnp.concatenate([rbuf[q, source, p * pool : (p + 1) * pool] for source in range(N_ORB)], axis=0)
                    for p in range(COLS // 128)
                ],
                axis=1,
            )
            res = jnp.dot(merge[pair], data, preferred_element_type=jnp.float32)
            for p in range(COLS // 128):
                a = res[:OCC, p * 128 : (p + 1) * 128]
                b = res[OCC:, p * 128 : (p + 1) * 128]
                even = jnp.where(low, a, pltpu.roll(b, 64, 1))
                odd = jnp.where(low, pltpu.roll(a, 64, 1), b)
                xbuf[pair, p * OCC : (p + 1) * OCC] = even.astype(jnp.bfloat16)
                xbuf[pair, ROWS + p * OCC : ROWS + (p + 1) * OCC] = odd.astype(jnp.bfloat16)

    def gram(r):
        left = jnp.concatenate([xbuf[2 * r], xbuf[2 * r + 1]], axis=1)
        for c in range(4):
            right = jnp.concatenate([xbuf[2 * c], xbuf[2 * c + 1]], axis=1)
            acc[r, :, c * 256 : (c + 1) * 256] += lax.dot_general(
                left, right, (((0,), (0,)), ((), ())), preferred_element_type=jnp.float32
            )

    @pl.loop(0, QS)
    def _(q):
        for t, other in enumerate(others):
            data_copy(q, t, other).wait_recv()
        spread(q)

        @pl.when(q < QS - 1)
        def _():
            @pl.loop(0, 4)
            def _(r):
                gram(r)

    for r in range(4):
        gram(r)
        gsend[r * 256 : (r + 1) * 256] = acc[r].astype(jnp.bfloat16)
        swap(r).start()
    for r in range(4):
        swap(r).wait_recv()
        for c in range(8):
            lanes = slice(c * 128, (c + 1) * 128)
            total = acc[r, :, lanes] + gpeer[r * 256 : (r + 1) * 256, lanes].astype(jnp.float32)
            turned = pltpu.roll(total, 64, 1)
            for i in range(4):
                rows = slice(i * TILE, (i + 1) * TILE)
                blocks[c * 17 + r * 4 + i] = total[rows].astype(jnp.bfloat16)
                blocks[(8 + c) * 17 + r * 4 + i] = turned[rows].astype(jnp.bfloat16)

    to_smem.wait()

    def block(yy, xx, zz, j):
        k = (yy * 4 + xx) * 32 + zz * 8 + core * 4 + 2 * j
        return jnp.where(low, blocks[index_smem[0, k]], blocks[index_smem[0, k + 1]])

    axes = ("xyz", "yzx", "zxy")

    def ring(part, stage, source, landing, steps=STEPS):
        axis = axes[part][stage]
        at = part * 3 + stage
        return [
            pltpu.make_async_remote_copy(
                src_ref=source.at[lax.rem(place[axis] + step, 4)],
                dst_ref=landing.at[3 - step],
                send_sem=ring_send.at[at, step - 1],
                recv_sem=ring_recv.at[at, 3 - step],
                device_id=along(axis, step),
                device_id_type=MESH,
            )
            for step in steps
        ]

    def begin(copies):
        for copy in copies:
            copy.start()
        return copies

    def arrive(copies):
        for copy in copies:
            copy.wait_recv()

    everything = []
    one = [[], [], []]
    for step in STEPS + (0,):
        xx = lax.rem(x + step, 4)

        @pl.loop(0, 16)
        def _(i):
            yy, zz = i // 4, lax.rem(i, 4)
            value = block(yy, xx, zz, 0)
            e_a[xx, yy, zz] = value[:CUT]
            e_c[zz, xx, yy, 0] = value[CUT:]

        if step:
            one[0] += begin(ring(0, 0, e_a, r1_a, (step,)))
        yy = lax.rem(y + step, 4)

        @pl.loop(0, 16)
        def _(i):
            zz, xx = i // 4, lax.rem(i, 4)
            value = block(yy, xx, zz, 1)
            e_b[yy, zz, xx] = value[:CUT]
            e_c[zz, xx, yy, 1] = value[CUT:]

        if step:
            one[1] += begin(ring(1, 0, e_b, r1_b, (step,)))
    one[2] = begin(ring(2, 0, e_c, r1_c))

    def total(part, stage, source, landing, i):
        at = place[axes[part][stage]]
        value = source[at, i].astype(jnp.float32)
        for n in range(3):
            value = value + landing[n, i].astype(jnp.float32)
        return value

    two, three = [], []
    for part, (e, r1, s2, r2) in enumerate(((e_a, r1_a, s2_a, r2_a), (e_b, r1_b, s2_b, r2_b), (e_c, r1_c, s2_c, r2_c))):
        arrive(one[part])
        for i in range(4):
            s2[i] = total(part, 0, e, r1, i).astype(jnp.bfloat16)
        two.append(begin(ring(part, 1, s2, r2)))
    for part, (s2, r2, s3, r3) in enumerate(((s2_a, r2_a, s3_a, r3_a), (s2_b, r2_b, s3_b, r3_b), (s2_c, r2_c, s3_c, r3_c))):
        arrive(two[part])
        for i in range(4):
            s3[i] = total(part, 1, s2, r2, i)
        three.append(begin(ring(part, 2, s3, r3)))

    for copy in tell_y:
        copy.wait_recv()
    found = jnp.max(row[...] + overs[1, 0] + overs[1, 1] + overs[1, 2])
    any_ref[0] = jnp.where(found > 0.5, 1, 0)

    for part, (s3, r3) in enumerate(((s3_a, r3_a), (s3_b, r3_b), (s3_c, r3_c))):
        arrive(three[part])
        value = s3[place[axes[part][2]]] + r3[0] + r3[1] + r3[2]
        if part < 2:
            done[part, :CUT] = value
        else:
            done[0, CUT:] = value[0]
            done[1, CUT:] = value[1]
    low = lax.broadcasted_iota(jnp.int32, (TILE // 2, 128), 1) < TILE
    for i in range(2):
        even = done[i, pl.ds(0, TILE // 2, stride=2), :]
        odd = done[i, pl.ds(1, TILE // 2, stride=2), :]
        left = jnp.where(low, even, pltpu.roll(odd, 64, 1))
        right = jnp.where(low, pltpu.roll(even, 64, 1), odd)
        for m in range(TILE // 2):
            out_ref[2 * i : 2 * i + 1, m * 128 : (m + 1) * 128] = left[m : m + 1]
            out_ref[2 * i + 1 : 2 * i + 2, m * 128 : (m + 1) * 128] = right[m : m + 1]

    for copies in one + two + three + [tell_x, tell_y]:
        for copy in copies:
            copy.wait_send()
    for r in range(4):
        swap(r).wait_send()
    for t in range(len(others)):
        mu_copy(t, me).wait_send()

    @pl.loop(0, QS)
    def _(q):
        for t in range(len(others)):
            data_copy(q, t, me).wait_send()


def exchange(pool, identity, mu, nu, live, support, coeffs, pair_mu, pair_nu, ints):
    dma = pltpu.SemaphoreType.DMA
    size = SLOTS * TILE
    bf16, f32 = jnp.bfloat16, jnp.float32
    first, second = (CUT, 128), (2, TILE - CUT, 128)

    def rings(lead, kind):
        return [pltpu.VMEM(lead + rest, kind) for rest in (first, first, second)]

    return pl.pallas_call(
        functools.partial(exchange_kernel, pool),
        out_shape=(
            jax.ShapeDtypeStruct((4, TILE * TILE), f32),
            jax.ShapeDtypeStruct((1,), jnp.int32),
        ),
        in_specs=[SMEM] * 3 + [VMEM] * 4 + [pl.BlockSpec(memory_space=pl.ANY)],
        out_specs=(VMEM, SMEM),
        scratch_shapes=[
            pltpu.VMEM((QS, 2, TILE, COLS * N_ORB), bf16),
            pltpu.VMEM((QS, N_ORB - 1, COLS // 128 * pool, 128), bf16),
            pltpu.VMEM((QS, N_ORB, COLS // 128 * pool, 128), bf16),
            pltpu.VMEM((N_ORB, 2 * ROWS, 128), bf16),
            pltpu.VMEM((SUP, OCC, 128), f32),
            pltpu.VMEM((N_ORB, 2 * OCC, 2 * OCC), f32),
            pltpu.VMEM((N_ORB, 2 * OCC, N_ORB * pool), bf16),
            pltpu.VMEM((N_ORB * pool, 128), f32),
            pltpu.VMEM((SLOTS, 128), jnp.int32),
            pltpu.VMEM((4, size // 4, size), f32),
            pltpu.VMEM((size, size), bf16),
            pltpu.VMEM((size, size), bf16),
            pltpu.VMEM((BLOCKS, TILE, 128), bf16),
            pltpu.VMEM((1, pair_mu.shape[1]), jnp.int32),
            pltpu.SMEM((1, pair_mu.shape[1]), jnp.int32),
            pltpu.VMEM((2, 8, 128), jnp.int32),
            pltpu.VMEM((N_ORB, 2, 8, 128), jnp.int32),
            pltpu.VMEM((8, 128), f32),
            pltpu.VMEM((8, 128), f32),
            pltpu.VMEM((2, 3, 8, 128), f32),
            pltpu.VMEM((2, TILE, 128), f32),
            *rings((4, 4, 4), bf16),
            *rings((3, 4, 4), bf16),
            *rings((4, 4), bf16),
            *rings((3, 4), bf16),
            *rings((4,), f32),
            *rings((3,), f32),
            dma((QS,)),
            dma((QS, N_ORB - 1)),
            dma((QS, N_ORB)),
            dma((N_ORB - 1,)),
            dma((N_ORB,)),
            dma((4,)),
            dma((4,)),
            dma(()),
            dma((2, 3)),
            dma((2, 3)),
            dma((9, 3)),
            dma((9, 3)),
        ],
        compiler_params=pltpu.CompilerParams(
            collective_id=identity, has_side_effects=True, vmem_limit_bytes=LIMIT
        ),
        name="exchange",
    )(mu, nu, live, support, coeffs, pair_mu, pair_nu, ints)


def on_device(integrals, tile_mu, tile_nu, live_count, support, coeffs, pair_mu, pair_nu):
    args = (tile_mu, tile_nu, live_count, support.T, coeffs, pair_mu[None, :], pair_nu[None, :], integrals)

    out, over = exchange(POOL, 0, *args)
    return lax.cond(over[0] == 0, lambda: out, lambda: exchange(2 * OCC, 1, *args)[0])


def solution(mesh):
    return jax.shard_map(
        on_device,
        mesh=mesh,
        in_specs=(
            P(("aux", "orb"), None, None),
            P(("aux", "orb")),
            P(("aux", "orb")),
            P(("aux", "orb")),
            P(),
            P(),
            P(),
            P(),
        ),
        out_specs=P(("aux", "orb"), None),
        check_vma=False,
    )
```

time: 93 us -> 77 us (0.83)
  Pallas kernels: 89.7 us -> 74.6 us
    pallas_call x3 -> x1, Pallas kernels: 89.7 us -> 74.6 us  [exchange(): pl.pallas_call(functools.partial(exchange_kernel, pool), out_shape=(jax.S...]
where the time goes in v3:
time: 77 us; the launch traced here: 76.8 us
  Pallas kernels  74.6 us (97%)
  between operations  1.39 us (2%)
    pallas_call x1, Pallas kernels, exchange(): pl.pallas_call(functools.partial(exchange_kernel, pool), out_shape=(jax.S...  74.6 us

profile of v3, /device:TPU:0, one launch (start us, length us, event | category | flops | bytes accessed | tf_op | source)
XLA Modules:
  0.0 76.8 jit_solution(3925468505451402866)
XLA Ops:
  0.0 0.0 copy-start
  0.0 0.0 copy-start.5
  0.0 0.0 copy-start.4
  0.0 0.0 copy-start.3
  0.0 0.0 copy-start.2
  0.0 0.0 copy-start.1
  0.7 74.6 %exchange.3 = (f32[4,4096]{1,0:T(4,128)S(1)}, s32[1]{0:T(128)}) custom-call(s32[2]{0:T(128)} %mu_ref.1, s32[2]{0:T(128)} %nu_ref.1, s32[1]{0:T(128)S(6)} %copy.14.live_ref, s32[16,64]{1,0:T(8,128)} %bitcast.4, bf16[64,1024]{1,0:T(8,128)(2,1)} %coeffs_ref.1, s32[1,512]{1,0:T(1,128)} %bitcast.6, s32[1,512]{1,0:T(1,128)} %bitcast.8, bf16[2,64,16384]{2,1,0:T(8,128)(2,1)} %ints_hbm.1), custom_call_target="tpu_custom_call" | custom-call | tf_op jit(solution)/shard_map/exchange/pallas_call | solution.py:493
  75.9 0.0 copy-done
  75.9 0.0 copy-done.5
  75.9 0.0 copy-done.4
  76.0 0.0 copy-done.3
  76.0 0.0 copy-done.2
  76.0 0.0 copy-done.1
  76.0 0.2 conditional.1
  76.2 0.6 copy.15
Async XLA Ops:
  0.0 75.9 %copy-start = (bf16[64,1024]{1,0:T(8,128)(2,1)S(1)}, bf16[64,1024]{1,0:T(8,128)(2,1)}, u32[]{:S(2)}) copy-start(bf16[64,1024]{1,0:T(8,128)(2,1)} %coeffs_ref.1) | copy-start | bytes 393220
  0.0 75.9 %copy-start.5 = (s32[2]{0:T(128)S(1)}, s32[2]{0:T(128)}, u32[]{:S(2)}) copy-start(s32[2]{0:T(128)} %nu_ref.1) | copy-start | bytes 28
  0.0 75.9 %copy-start.4 = (s32[2]{0:T(128)S(1)}, s32[2]{0:T(128)}, u32[]{:S(2)}) copy-start(s32[2]{0:T(128)} %mu_ref.1) | copy-start | bytes 28
  0.0 75.9 %copy-start.3 = (s32[512]{0:T(512)S(1)}, s32[512]{0:T(512)}, u32[]{:S(2)}) copy-start(s32[512]{0:T(512)} %param.17) | copy-start | bytes 6148
  0.0 76.0 %copy-start.2 = (s32[512]{0:T(512)S(1)}, s32[512]{0:T(512)}, u32[]{:S(2)}) copy-start(s32[512]{0:T(512)} %param.16) | copy-start | bytes 6148
  0.0 76.0 %copy-start.1 = (s32[64,16]{0,1:T(8,128)S(1)}, s32[64,16]{0,1:T(8,128)}, u32[]{:S(2)}) copy-start(s32[64,16]{0,1:T(8,128)} %param.14) | copy-start | bytes 12292

commit v4 on v3

--- a/solution.py
+++ b/solution.py
@@ -13,7 +13,7 @@
 SUP = 16
 WT = 32
 N_ORB = 8
-POOL = 96
+POOL = 88
 SLOTS = 16
 QS = 4
 COLS = AUX_DEV * TILE // (QS * N_ORB)
@@ -29,6 +29,11 @@
 
 STEPS = (2, 1, 3)
 BLOCKS = 17 * 16
+
+
+def chunk_rows(pool):
+    top = pool // 16 * 16
+    return top, COLS // 128 * top, COLS // 128 * top + (COLS // 256 * 16 if pool > top else 0)
 
 
 def exchange_kernel(
@@ -95,6 +100,8 @@
     ring_send,
     ring_recv,
 ):
+    top, tops, _ = chunk_rows(pool)
+    ragged = pool > top
     aux = lax.axis_index("aux")
     me = lax.axis_index("orb")
     y, x = aux // 4, lax.rem(aux, 4)
@@ -209,9 +216,13 @@
 
     def products(q, dest, store):
         block = ints[q, :, :, pl.ds(pl.multiple_of(dest * COLS, COLS), COLS)].reshape(2 * TILE, COLS)
-        res = jnp.dot(packed, block, preferred_element_type=jnp.float32).astype(jnp.bfloat16)
+        res = jnp.dot(packed, block, preferred_element_type=jnp.float32)
         for p in range(COLS // 128):
-            store(p * pool, res[:, p * 128 : (p + 1) * 128])
+            store(p * top, res[:top, p * 128 : (p + 1) * 128].astype(jnp.bfloat16))
+        if ragged:
+            for p in range(0, COLS // 128, 2):
+                last = [res[top:, (p + i) * 128 : (p + i + 1) * 128] for i in range(2)]
+                store(tops + p * 8, jnp.concatenate(last, axis=0).astype(jnp.bfloat16))
 
     def tell(stage, axis, source):
         return [
@@ -236,13 +247,13 @@
         for t, other in enumerate(others):
 
             def to_send(row, value):
-                sbuf[q, t, row : row + pool, :] = value
+                sbuf[q, t, row : row + value.shape[0], :] = value
 
             products(q, other, to_send)
             data_copy(q, t, me).start()
 
         def to_own(row, value):
-            rbuf[q, me, row : row + pool, :] = value
+            rbuf[q, me, row : row + value.shape[0], :] = value
 
         products(q, me, to_own)
 
@@ -270,6 +281,8 @@
             is_first = jnp.where(mu_of(t) == mu_of(s), 0, is_first)
         first[s : s + 1] = jnp.where(mu_of(s) >= 0, is_first, 0)
     low_row = low[:1]
+    if ragged:
+        stack[N_ORB * top :] = jnp.zeros((N_ORB * 16, 128), jnp.float32)
     for pair in range(N_ORB):
 
         @pl.loop(0, N_ORB)
@@ -282,10 +295,17 @@
             turned = jnp.where(low_row, shares(2 * pair, 1), shares(2 * pair + 1, 0))
             placed = unpack[source]
             both = placed * kept + pltpu.roll(placed, 64, 1) * turned
-            at_row = pl.ds(pl.multiple_of(source * pool, pool), pool)
-            stack[at_row] = both[:pool]
-
-        merge[pair] = stack[...].T.astype(jnp.bfloat16)
+            stack[pl.ds(pl.multiple_of(source * top, top), top)] = both[:top]
+            if ragged:
+                stack[pl.ds(pl.multiple_of(N_ORB * top + source * 16, 16), 8)] = both[top:pool]
+
+        merged = stack[...].T
+        at = slice(pair % 4 * 128, (pair % 4 + 1) * 128)
+        merge[0, pair // 4, at] = merged.astype(jnp.bfloat16)
+        if ragged:
+            turned = pltpu.roll(merged[:, N_ORB * top :], 8, 1)
+            merged = jnp.concatenate([merged[:, : N_ORB * top], turned], axis=1)
+            merge[1, pair // 4, at] = merged.astype(jnp.bfloat16)
 
     k = lax.broadcasted_iota(jnp.int32, pm_ref.shape, 1)
     u = jnp.full(pm_ref.shape, SLOTS, jnp.int32)
@@ -313,23 +333,26 @@
     acc[...] = jnp.zeros_like(acc)
 
     def spread(q):
-        @pl.loop(0, N_ORB)
-        def _(pair):
-            data = jnp.concatenate(
-                [
-                    jnp.concatenate([rbuf[q, source, p * pool : (p + 1) * pool] for source in range(N_ORB)], axis=0)
-                    for p in range(COLS // 128)
-                ],
-                axis=1,
-            )
-            res = jnp.dot(merge[pair], data, preferred_element_type=jnp.float32)
-            for p in range(COLS // 128):
-                a = res[:OCC, p * 128 : (p + 1) * 128]
-                b = res[OCC:, p * 128 : (p + 1) * 128]
-                even = jnp.where(low, a, pltpu.roll(b, 64, 1))
-                odd = jnp.where(low, pltpu.roll(a, 64, 1), b)
-                xbuf[pair, p * OCC : (p + 1) * OCC] = even.astype(jnp.bfloat16)
-                xbuf[pair, ROWS + p * OCC : ROWS + (p + 1) * OCC] = odd.astype(jnp.bfloat16)
+        def column(p):
+            parts = [rbuf[q, source, p * top : (p + 1) * top] for source in range(N_ORB)]
+            if ragged:
+                at = tops + p // 2 * 16
+                parts += [rbuf[q, source, at : at + 16] for source in range(N_ORB)]
+            return jnp.concatenate(parts, axis=0)
+
+        for odd_p in range(2):
+            data = jnp.concatenate([column(p) for p in range(odd_p, COLS // 128, 2)], axis=1)
+            for half in range(2):
+                res = jnp.dot(merge[odd_p if ragged else 0, half], data, preferred_element_type=jnp.float32)
+                for n, p in enumerate(range(odd_p, COLS // 128, 2)):
+                    lanes = slice(n * 128, (n + 1) * 128)
+                    for i in range(4):
+                        a = res[i * 128 : i * 128 + OCC, lanes]
+                        b = res[i * 128 + OCC : (i + 1) * 128, lanes]
+                        even = jnp.where(low, a, pltpu.roll(b, 64, 1))
+                        odd = jnp.where(low, pltpu.roll(a, 64, 1), b)
+                        xbuf[half * 4 + i, p * OCC : (p + 1) * OCC] = even.astype(jnp.bfloat16)
+                        xbuf[half * 4 + i, ROWS + p * OCC : ROWS + (p + 1) * OCC] = odd.astype(jnp.bfloat16)
 
     def gram(r):
         left = jnp.concatenate([xbuf[2 * r], xbuf[2 * r + 1]], axis=1)
@@ -482,6 +505,8 @@
 
 
 def exchange(pool, identity, mu, nu, live, support, coeffs, pair_mu, pair_nu, ints):
+    top, _, rows = chunk_rows(pool)
+    depth = N_ORB * (top + (16 if pool > top else 0))
     dma = pltpu.SemaphoreType.DMA
     size = SLOTS * TILE
     bf16, f32 = jnp.bfloat16, jnp.float32
@@ -500,13 +525,13 @@
         out_specs=(VMEM, SMEM),
         scratch_shapes=[
             pltpu.VMEM((QS, 2, TILE, COLS * N_ORB), bf16),
-            pltpu.VMEM((QS, N_ORB - 1, COLS // 128 * pool, 128), bf16),
-            pltpu.VMEM((QS, N_ORB, COLS // 128 * pool, 128), bf16),
+            pltpu.VMEM((QS, N_ORB - 1, rows, 128), bf16),
+            pltpu.VMEM((QS, N_ORB, rows, 128), bf16),
             pltpu.VMEM((N_ORB, 2 * ROWS, 128), bf16),
             pltpu.VMEM((SUP, OCC, 128), f32),
             pltpu.VMEM((N_ORB, 2 * OCC, 2 * OCC), f32),
-            pltpu.VMEM((N_ORB, 2 * OCC, N_ORB * pool), bf16),
-            pltpu.VMEM((N_ORB * pool, 128), f32),
+            pltpu.VMEM((2 if pool > top else 1, 2, 8 * OCC, depth), bf16),
+            pltpu.VMEM((depth, 128), f32),
             pltpu.VMEM((SLOTS, 128), jnp.int32),
             pltpu.VMEM((4, size // 4, size), f32),
             pltpu.VMEM((size, size), bf16),

time: 77 us -> 72.4 us (0.940)
  Pallas kernels: 74.6 us -> 70 us
    pallas_call x1, Pallas kernels: 74.6 us -> 70 us  [exchange(): pl.pallas_call(functools.partial(exchange_kernel, pool), out_shape=(jax.S...]
where the time goes in v4:
time: 72.4 us; the launch traced here: 72.2 us
  Pallas kernels  70 us (97%)
  between operations  1.39 us (2%)
    pallas_call x1, Pallas kernels, exchange(): pl.pallas_call(functools.partial(exchange_kernel, pool), out_shape=(jax.S...  70 us

profile of v4, /device:TPU:0, one launch (start us, length us, event | category | flops | bytes accessed | tf_op | source)
XLA Modules:
  0.0 72.2 jit_solution(7282340571542917609)
XLA Ops:
  0.0 0.0 copy-start
  0.0 0.0 copy-start.5
  0.0 0.0 copy-start.4
  0.0 0.0 copy-start.3
  0.0 0.0 copy-start.2
  0.0 0.0 copy-start.1
  0.7 70.0 %exchange.3 = (f32[4,4096]{1,0:T(4,128)S(1)}, s32[1]{0:T(128)}) custom-call(s32[2]{0:T(128)} %mu_ref.1, s32[2]{0:T(128)} %nu_ref.1, s32[1]{0:T(128)S(6)} %copy.14.live_ref, s32[16,64]{1,0:T(8,128)} %bitcast.4, bf16[64,1024]{1,0:T(8,128)(2,1)} %coeffs_ref.1, s32[1,512]{1,0:T(1,128)} %bitcast.6, s32[1,512]{1,0:T(1,128)} %bitcast.8, bf16[2,64,16384]{2,1,0:T(8,128)(2,1)} %ints_hbm.1), custom_call_target="tpu_custom_call" | custom-call | tf_op jit(solution)/shard_map/exchange/pallas_call | solution.py:518
  71.3 0.0 copy-done
  71.4 0.0 copy-done.5
  71.4 0.0 copy-done.4
  71.4 0.0 copy-done.3
  71.4 0.0 copy-done.2
  71.4 0.0 copy-done.1
  71.4 0.2 conditional.1
  71.6 0.6 copy.15
Async XLA Ops:
  0.0 71.3 %copy-start = (bf16[64,1024]{1,0:T(8,128)(2,1)S(1)}, bf16[64,1024]{1,0:T(8,128)(2,1)}, u32[]{:S(2)}) copy-start(bf16[64,1024]{1,0:T(8,128)(2,1)} %coeffs_ref.1) | copy-start | bytes 393220
  0.0 71.4 %copy-start.5 = (s32[2]{0:T(128)S(1)}, s32[2]{0:T(128)}, u32[]{:S(2)}) copy-start(s32[2]{0:T(128)} %nu_ref.1) | copy-start | bytes 28
  0.0 71.4 %copy-start.4 = (s32[2]{0:T(128)S(1)}, s32[2]{0:T(128)}, u32[]{:S(2)}) copy-start(s32[2]{0:T(128)} %mu_ref.1) | copy-start | bytes 28
  0.0 71.4 %copy-start.3 = (s32[512]{0:T(512)S(1)}, s32[512]{0:T(512)}, u32[]{:S(2)}) copy-start(s32[512]{0:T(512)} %param.17) | copy-start | bytes 6148
  0.0 71.4 %copy-start.2 = (s32[512]{0:T(512)S(1)}, s32[512]{0:T(512)}, u32[]{:S(2)}) copy-start(s32[512]{0:T(512)} %param.16) | copy-start | bytes 6148
  0.0 71.4 %copy-start.1 = (s32[64,16]{0,1:T(8,128)S(1)}, s32[64,16]{0,1:T(8,128)}, u32[]{:S(2)}) copy-start(s32[64,16]{0,1:T(8,128)} %param.14) | copy-start | bytes 12292

commit v5 on v4

--- a/solution.py
+++ b/solution.py
@@ -14,11 +14,12 @@
 WT = 32
 N_ORB = 8
 POOL = 88
+NPAIR = 512
 SLOTS = 16
 QS = 4
 COLS = AUX_DEV * TILE // (QS * N_ORB)
 ROWS = COLS // 128 * OCC
-CUT = 48
+CAP = 20
 MESH = pl.DeviceIdType.MESH
 VMEM = pl.BlockSpec(memory_space=pltpu.VMEM)
 SMEM = pl.BlockSpec(memory_space=pltpu.SMEM)
@@ -28,7 +29,6 @@
 
 
 STEPS = (2, 1, 3)
-BLOCKS = 17 * 16
 
 
 def chunk_rows(pool):
@@ -38,6 +38,7 @@
 
 def exchange_kernel(
     pool,
+    cap,
     mu_ref,
     nu_ref,
     live_ref,
@@ -58,10 +59,9 @@
     stack,
     first,
     acc,
-    gsend,
-    gpeer,
-    blocks,
+    order,
     index,
+    order_smem,
     index_smem,
     mine,
     mus,
@@ -69,24 +69,20 @@
     row,
     overs,
     done,
+    gsend,
+    gpeer,
+    kept_tiles,
+    sz,
+    rz,
+    blocks,
     e_a,
     e_b,
-    e_c,
     r1_a,
     r1_b,
-    r1_c,
     s2_a,
     s2_b,
-    s2_c,
     r2_a,
     r2_b,
-    r2_c,
-    s3_a,
-    s3_b,
-    s3_c,
-    r3_a,
-    r3_b,
-    r3_c,
     in_sem,
     send_sem,
     recv_sem,
@@ -94,6 +90,7 @@
     mu_recv,
     g_send,
     g_recv,
+    order_sem,
     index_sem,
     tell_send,
     tell_recv,
@@ -102,6 +99,7 @@
 ):
     top, tops, _ = chunk_rows(pool)
     ragged = pool > top
+    lists = order.shape[1]
     aux = lax.axis_index("aux")
     me = lax.axis_index("orb")
     y, x = aux // 4, lax.rem(aux, 4)
@@ -203,13 +201,13 @@
             device_id_type=MESH,
         )
 
-    def swap(r):
-        rows = pl.ds(r * 256, 256)
+    def swap(step):
+        zz = lax.rem(z + step, 4)
         return pltpu.make_async_remote_copy(
-            src_ref=gsend.at[rows],
-            dst_ref=gpeer.at[rows],
-            send_sem=g_send.at[r],
-            recv_sem=g_recv.at[r],
+            src_ref=gsend.at[zz],
+            dst_ref=gpeer.at[zz],
+            send_sem=g_send.at[step],
+            recv_sem=g_recv.at[step],
             device_id=(aux, peer),
             device_id_type=MESH,
         )
@@ -268,10 +266,6 @@
         unpack[source] = placed.astype(jnp.float32).T
         over[...] = jnp.maximum(over[...], jnp.where(rows > pool, 1.0, 0.0))
 
-    tell_x = tell(0, "x", over)
-    for copy in tell_x:
-        copy.start()
-
     def mu_of(slot):
         return mus[slot // 2, 0, slot % 2 : slot % 2 + 1]
 
@@ -308,21 +302,41 @@
             merge[1, pair // 4, at] = merged.astype(jnp.bfloat16)
 
     k = lax.broadcasted_iota(jnp.int32, pm_ref.shape, 1)
-    u = jnp.full(pm_ref.shape, SLOTS, jnp.int32)
+    u = jnp.full(pm_ref.shape, -1, jnp.int32)
     v = jnp.full(pm_ref.shape, -1, jnp.int32)
     for s in range(SLOTS):
         known = first[s : s + 1, :1] > 0
         tile = mu_of(s)[:, :1]
         u = jnp.where(jnp.logical_and(known, pm_ref[...] == tile), s, u)
         v = jnp.where(jnp.logical_and(known, pn_ref[...] == tile), s, v)
-    u = jnp.where(v >= 0, u, SLOTS)
-    v = jnp.maximum(v, 0)
-    index[...] = (((v + k) & 1) * 8 + (v >> 1)) * 17 + u
-    to_smem = pltpu.make_async_copy(index, index_smem, index_sem)
-    to_smem.start()
-    for c in range(16):
-        blocks[c * 17 + 16] = jnp.zeros((TILE, 128), jnp.bfloat16)
-
+    active = jnp.logical_and(u >= 0, v >= 0)
+    npair = pm_ref.shape[1]
+    square = (npair, npair)
+    to, at = lax.broadcasted_iota(jnp.int32, square, 0), lax.broadcasted_iota(jnp.int32, square, 1)
+    ahead = jnp.where(jnp.logical_and(to < at, ((to ^ at) & 28) == 0), 1.0, 0.0).astype(jnp.bfloat16)
+    flags = jnp.broadcast_to(jnp.where(active, 1.0, 0.0), (8, npair)).astype(jnp.bfloat16)
+    rank = jnp.dot(flags, ahead, preferred_element_type=jnp.float32)[:1].astype(jnp.int32)
+    spill = jnp.logical_and(active, rank >= cap)
+    over[...] = jnp.maximum(over[...], jnp.max(jnp.where(spill, 1.0, 0.0)))
+    listed = jnp.logical_and(active, rank < cap)
+    at_list = jnp.where(listed, ((k >> 2) & 7) * cap + rank, -1)
+    chosen = jnp.where(lax.broadcasted_iota(jnp.int32, (lists, npair), 0) == at_list, 1.0, 0.0)
+    tiles_of = jnp.broadcast_to((u * SLOTS + v).astype(jnp.float32), (8, npair)).astype(jnp.bfloat16)
+    order[...] = lax.dot_general(
+        tiles_of, chosen.astype(jnp.bfloat16), (((1,), (1,)), ((), ())), preferred_element_type=jnp.float32
+    )[:1].astype(jnp.int32)
+    index[...] = jnp.where(listed, ((rank + k) & 1) * (cap // 2 + 1) + (rank >> 1), cap // 2)
+    to_smem = [
+        pltpu.make_async_copy(order, order_smem, order_sem),
+        pltpu.make_async_copy(index, index_smem, index_sem),
+    ]
+    for copy in to_smem:
+        copy.start()
+    blocks[cap // 2] = jnp.zeros((TILE, 128), jnp.bfloat16)
+
+    tell_x = tell(0, "x", over)
+    for copy in tell_x:
+        copy.start()
     for copy in tell_x:
         copy.wait_recv()
     row[...] = over[...] + overs[0, 0] + overs[0, 1] + overs[0, 2]
@@ -358,9 +372,12 @@
         left = jnp.concatenate([xbuf[2 * r], xbuf[2 * r + 1]], axis=1)
         for c in range(4):
             right = jnp.concatenate([xbuf[2 * c], xbuf[2 * c + 1]], axis=1)
-            acc[r, :, c * 256 : (c + 1) * 256] += lax.dot_general(
+            res = lax.dot_general(
                 left, right, (((0,), (0,)), ((), ())), preferred_element_type=jnp.float32
             )
+            for i in range(4):
+                for h in range(2):
+                    acc[(r * 4 + i) * 8 + c * 2 + h] += res[i * TILE : (i + 1) * TILE, h * 128 : (h + 1) * 128]
 
     @pl.loop(0, QS)
     def _(q):
@@ -368,118 +385,119 @@
             data_copy(q, t, other).wait_recv()
         spread(q)
 
-        @pl.when(q < QS - 1)
-        def _():
-            @pl.loop(0, 4)
-            def _(r):
-                gram(r)
-
-    for r in range(4):
-        gram(r)
-        gsend[r * 256 : (r + 1) * 256] = acc[r].astype(jnp.bfloat16)
-        swap(r).start()
-    for r in range(4):
-        swap(r).wait_recv()
-        for c in range(8):
-            lanes = slice(c * 128, (c + 1) * 128)
-            total = acc[r, :, lanes] + gpeer[r * 256 : (r + 1) * 256, lanes].astype(jnp.float32)
-            turned = pltpu.roll(total, 64, 1)
-            for i in range(4):
-                rows = slice(i * TILE, (i + 1) * TILE)
-                blocks[c * 17 + r * 4 + i] = total[rows].astype(jnp.bfloat16)
-                blocks[(8 + c) * 17 + r * 4 + i] = turned[rows].astype(jnp.bfloat16)
-
-    to_smem.wait()
-
-    def block(yy, xx, zz, j):
-        k = (yy * 4 + xx) * 32 + zz * 8 + core * 4 + 2 * j
-        return jnp.where(low, blocks[index_smem[0, k]], blocks[index_smem[0, k + 1]])
-
-    axes = ("xyz", "yzx", "zxy")
-
-    def ring(part, stage, source, landing, steps=STEPS):
-        axis = axes[part][stage]
-        at = part * 3 + stage
-        return [
-            pltpu.make_async_remote_copy(
-                src_ref=source.at[lax.rem(place[axis] + step, 4)],
-                dst_ref=landing.at[3 - step],
-                send_sem=ring_send.at[at, step - 1],
-                recv_sem=ring_recv.at[at, 3 - step],
-                device_id=along(axis, step),
-                device_id_type=MESH,
-            )
-            for step in steps
-        ]
-
-    def begin(copies):
-        for copy in copies:
-            copy.start()
-        return copies
-
-    def arrive(copies):
+        @pl.loop(0, 4)
+        def _(r):
+            gram(r)
+
+    for copy in to_smem:
+        copy.wait()
+
+    def ring(part, stage, axis, source, landing, step):
+        at = part * 2 + stage
+        return pltpu.make_async_remote_copy(
+            src_ref=source.at[lax.rem(place[axis] + step, 4)],
+            dst_ref=landing.at[3 - step],
+            send_sem=ring_send.at[at, step - 1],
+            recv_sem=ring_recv.at[at, 3 - step],
+            device_id=along(axis, step),
+            device_id_type=MESH,
+        )
+
+    def started(copy):
+        copy.start()
+        return copy
+
+    def packed_tiles(owner, b):
+        at = owner * cap + 2 * b
+        t0, t1 = order_smem[0, at] & 255, order_smem[0, at + 1] & 255
+        tile0, tile1 = acc[t0 >> 1], acc[t1 >> 1]
+        in_place = jnp.broadcast_to(jnp.where(low_row, t0 & 1, 1 - (t1 & 1)), low.shape) == 0
+        straight, crossed = jnp.where(low, tile0, tile1), jnp.where(low, tile1, tile0)
+        return jnp.where(in_place, straight, pltpu.roll(crossed, 64, 1))
+
+    unroll = 10 if cap % 10 == 0 else 4
+
+    def give(step):
+        zz = lax.rem(z + step, 4)
+
+        @pl.loop(0, cap // 2, unroll=unroll)
+        def _(b):
+            gsend[zz, b] = packed_tiles(zz * 2 + 1 - core, b).astype(jnp.bfloat16)
+
+        swap(step).start()
+
+    z_copies = []
+
+    def take(step):
+        zz = lax.rem(z + step, 4)
+
+        @pl.loop(0, cap // 2, unroll=unroll)
+        def _(b):
+            kept_tiles[b] = packed_tiles(zz * 2 + core, b)
+
+        swap(step).wait_recv()
+        sz[zz] = (kept_tiles[...] + gpeer[zz].astype(jnp.float32)).astype(jnp.bfloat16)
+        if step:
+            z_copies.append(started(ring(2, 0, "z", sz, rz, step)))
+
+    turns = STEPS + (0,)
+    give(turns[0])
+    for i in range(4):
+        if i < 3:
+            give(turns[i + 1])
+        take(turns[i])
+
+    for copy in z_copies:
+        copy.wait_recv()
+    for b in range(cap // 2):
+        total = sz[z, b].astype(jnp.float32)
+        for n in range(3):
+            total = total + rz[n, b].astype(jnp.float32)
+        blocks[b] = total.astype(jnp.bfloat16)
+        blocks[cap // 2 + 1 + b] = pltpu.roll(total, 64, 1).astype(jnp.bfloat16)
+
+    def block(yy, xx, j):
+        k = (yy * 4 + xx) * 32 + z * 8 + core * 4 + 2 * j
+        left, right = (jnp.clip(index_smem[0, k + h], 0, cap + 1) for h in range(2))
+        return jnp.where(low, blocks[left], blocks[right])
+
+    one_a, one_b = [], []
+    for step in turns:
+        xx, yy = lax.rem(x + step, 4), lax.rem(y + step, 4)
+        for i in range(4):
+            e_a[xx, i] = block(i, xx, 0)
+        if step:
+            one_a.append(started(ring(0, 0, "x", e_a, r1_a, step)))
+        for i in range(4):
+            e_b[yy, i] = block(yy, i, 1)
+        if step:
+            one_b.append(started(ring(1, 0, "y", e_b, r1_b, step)))
+
+    two = []
+    for part, copies, axis, then, e, r1, s2, r2 in (
+        (0, one_a, "x", "y", e_a, r1_a, s2_a, r2_a),
+        (1, one_b, "y", "x", e_b, r1_b, s2_b, r2_b),
+    ):
         for copy in copies:
             copy.wait_recv()
-
-    everything = []
-    one = [[], [], []]
-    for step in STEPS + (0,):
-        xx = lax.rem(x + step, 4)
-
-        @pl.loop(0, 16)
-        def _(i):
-            yy, zz = i // 4, lax.rem(i, 4)
-            value = block(yy, xx, zz, 0)
-            e_a[xx, yy, zz] = value[:CUT]
-            e_c[zz, xx, yy, 0] = value[CUT:]
-
-        if step:
-            one[0] += begin(ring(0, 0, e_a, r1_a, (step,)))
-        yy = lax.rem(y + step, 4)
-
-        @pl.loop(0, 16)
-        def _(i):
-            zz, xx = i // 4, lax.rem(i, 4)
-            value = block(yy, xx, zz, 1)
-            e_b[yy, zz, xx] = value[:CUT]
-            e_c[zz, xx, yy, 1] = value[CUT:]
-
-        if step:
-            one[1] += begin(ring(1, 0, e_b, r1_b, (step,)))
-    one[2] = begin(ring(2, 0, e_c, r1_c))
-
-    def total(part, stage, source, landing, i):
-        at = place[axes[part][stage]]
-        value = source[at, i].astype(jnp.float32)
-        for n in range(3):
-            value = value + landing[n, i].astype(jnp.float32)
-        return value
-
-    two, three = [], []
-    for part, (e, r1, s2, r2) in enumerate(((e_a, r1_a, s2_a, r2_a), (e_b, r1_b, s2_b, r2_b), (e_c, r1_c, s2_c, r2_c))):
-        arrive(one[part])
-        for i in range(4):
-            s2[i] = total(part, 0, e, r1, i).astype(jnp.bfloat16)
-        two.append(begin(ring(part, 1, s2, r2)))
-    for part, (s2, r2, s3, r3) in enumerate(((s2_a, r2_a, s3_a, r3_a), (s2_b, r2_b, s3_b, r3_b), (s2_c, r2_c, s3_c, r3_c))):
-        arrive(two[part])
-        for i in range(4):
-            s3[i] = total(part, 1, s2, r2, i)
-        three.append(begin(ring(part, 2, s3, r3)))
+        for step in turns:
+            i = lax.rem(place[then] + step, 4)
+            total = e[place[axis], i].astype(jnp.float32)
+            for n in range(3):
+                total = total + r1[n, i].astype(jnp.float32)
+            s2[i] = total
+            if step:
+                two.append(started(ring(part, 1, then, s2, r2, step)))
 
     for copy in tell_y:
         copy.wait_recv()
     found = jnp.max(row[...] + overs[1, 0] + overs[1, 1] + overs[1, 2])
     any_ref[0] = jnp.where(found > 0.5, 1, 0)
 
-    for part, (s3, r3) in enumerate(((s3_a, r3_a), (s3_b, r3_b), (s3_c, r3_c))):
-        arrive(three[part])
-        value = s3[place[axes[part][2]]] + r3[0] + r3[1] + r3[2]
-        if part < 2:
-            done[part, :CUT] = value
-        else:
-            done[0, CUT:] = value[0]
-            done[1, CUT:] = value[1]
+    for part, then, s2, r2 in ((0, "y", s2_a, r2_a), (1, "x", s2_b, r2_b)):
+        for copy in two[part * 3 : part * 3 + 3]:
+            copy.wait_recv()
+        done[part] = s2[place[then]] + r2[0] + r2[1] + r2[2]
     low = lax.broadcasted_iota(jnp.int32, (TILE // 2, 128), 1) < TILE
     for i in range(2):
         even = done[i, pl.ds(0, TILE // 2, stride=2), :]
@@ -490,11 +508,10 @@
             out_ref[2 * i : 2 * i + 1, m * 128 : (m + 1) * 128] = left[m : m + 1]
             out_ref[2 * i + 1 : 2 * i + 2, m * 128 : (m + 1) * 128] = right[m : m + 1]
 
-    for copies in one + two + three + [tell_x, tell_y]:
-        for copy in copies:
-            copy.wait_send()
-    for r in range(4):
-        swap(r).wait_send()
+    for copy in z_copies + one_a + one_b + two + tell_x + tell_y:
+        copy.wait_send()
+    for step in range(4):
+        swap(step).wait_send()
     for t in range(len(others)):
         mu_copy(t, me).wait_send()
 
@@ -504,19 +521,16 @@
             data_copy(q, t, me).wait_send()
 
 
-def exchange(pool, identity, mu, nu, live, support, coeffs, pair_mu, pair_nu, ints):
+def exchange(pool, cap, identity, mu, nu, live, support, coeffs, pair_mu, pair_nu, ints):
     top, _, rows = chunk_rows(pool)
     depth = N_ORB * (top + (16 if pool > top else 0))
     dma = pltpu.SemaphoreType.DMA
-    size = SLOTS * TILE
     bf16, f32 = jnp.bfloat16, jnp.float32
-    first, second = (CUT, 128), (2, TILE - CUT, 128)
-
-    def rings(lead, kind):
-        return [pltpu.VMEM(lead + rest, kind) for rest in (first, first, second)]
+    half = cap // 2
+    lists = pl.cdiv(N_ORB * cap, 128) * 128
 
     return pl.pallas_call(
-        functools.partial(exchange_kernel, pool),
+        functools.partial(exchange_kernel, pool, cap),
         out_shape=(
             jax.ShapeDtypeStruct((4, TILE * TILE), f32),
             jax.ShapeDtypeStruct((1,), jnp.int32),
@@ -533,11 +547,10 @@
             pltpu.VMEM((2 if pool > top else 1, 2, 8 * OCC, depth), bf16),
             pltpu.VMEM((depth, 128), f32),
             pltpu.VMEM((SLOTS, 128), jnp.int32),
-            pltpu.VMEM((4, size // 4, size), f32),
-            pltpu.VMEM((size, size), bf16),
-            pltpu.VMEM((size, size), bf16),
-            pltpu.VMEM((BLOCKS, TILE, 128), bf16),
+            pltpu.VMEM((SLOTS * SLOTS // 2, TILE, 128), f32),
+            pltpu.VMEM((1, lists), jnp.int32),
             pltpu.VMEM((1, pair_mu.shape[1]), jnp.int32),
+            pltpu.SMEM((1, lists), jnp.int32),
             pltpu.SMEM((1, pair_mu.shape[1]), jnp.int32),
             pltpu.VMEM((2, 8, 128), jnp.int32),
             pltpu.VMEM((N_ORB, 2, 8, 128), jnp.int32),
@@ -545,12 +558,20 @@
             pltpu.VMEM((8, 128), f32),
             pltpu.VMEM((2, 3, 8, 128), f32),
             pltpu.VMEM((2, TILE, 128), f32),
-            *rings((4, 4, 4), bf16),
-            *rings((3, 4, 4), bf16),
-            *rings((4, 4), bf16),
-            *rings((3, 4), bf16),
-            *rings((4,), f32),
-            *rings((3,), f32),
+            pltpu.VMEM((4, half, TILE, 128), bf16),
+            pltpu.VMEM((4, half, TILE, 128), bf16),
+            pltpu.VMEM((half, TILE, 128), f32),
+            pltpu.VMEM((4, half, TILE, 128), bf16),
+            pltpu.VMEM((3, half, TILE, 128), bf16),
+            pltpu.VMEM((cap + 2, TILE, 128), bf16),
+            pltpu.VMEM((4, 4, TILE, 128), bf16),
+            pltpu.VMEM((4, 4, TILE, 128), bf16),
+            pltpu.VMEM((3, 4, TILE, 128), bf16),
+            pltpu.VMEM((3, 4, TILE, 128), bf16),
+            pltpu.VMEM((4, TILE, 128), f32),
+            pltpu.VMEM((4, TILE, 128), f32),
+            pltpu.VMEM((3, TILE, 128), f32),
+            pltpu.VMEM((3, TILE, 128), f32),
             dma((QS,)),
             dma((QS, N_ORB - 1)),
             dma((QS, N_ORB)),
@@ -559,10 +580,11 @@
             dma((4,)),
             dma((4,)),
             dma(()),
+            dma(()),
             dma((2, 3)),
             dma((2, 3)),
-            dma((9, 3)),
-            dma((9, 3)),
+            dma((5, 3)),
+            dma((5, 3)),
         ],
         compiler_params=pltpu.CompilerParams(
             collective_id=identity, has_side_effects=True, vmem_limit_bytes=LIMIT
@@ -574,8 +596,8 @@
 def on_device(integrals, tile_mu, tile_nu, live_count, support, coeffs, pair_mu, pair_nu):
     args = (tile_mu, tile_nu, live_count, support.T, coeffs, pair_mu[None, :], pair_nu[None, :], integrals)
 
-    out, over = exchange(POOL, 0, *args)
-    return lax.cond(over[0] == 0, lambda: out, lambda: exchange(2 * OCC, 1, *args)[0])
+    out, over = exchange(POOL, CAP, 0, *args)
+    return lax.cond(over[0] == 0, lambda: out, lambda: exchange(2 * OCC, NPAIR // N_ORB, 1, *args)[0])
 
 
 def solution(mesh):

time: 72.4 us -> 69.6 us (0.961)
  Pallas kernels: 70 us -> 67.2 us
    pallas_call x1, Pallas kernels: 70 us -> 67.2 us  [exchange(): pl.pallas_call(functools.partial(exchange_kernel, pool, cap), out_shape=(...]
where the time goes in v5:
time: 69.6 us; the launch traced here: 69.4 us
  Pallas kernels  67.2 us (97%)
  between operations  1.39 us (2%)
    pallas_call x1, Pallas kernels, exchange(): pl.pallas_call(functools.partial(exchange_kernel, pool, cap), out_shape=(...  67.2 us

profile of v5, /device:TPU:0, one launch (start us, length us, event | category | flops | bytes accessed | tf_op | source)
XLA Modules:
  0.0 69.4 jit_solution(16604888562294773171)
XLA Ops:
  0.0 0.0 copy-start
  0.0 0.0 copy-start.5
  0.0 0.0 copy-start.4
  0.0 0.0 copy-start.3
  0.0 0.0 copy-start.2
  0.0 0.0 copy-start.1
  0.7 67.2 %exchange.3 = (f32[4,4096]{1,0:T(4,128)S(1)}, s32[1]{0:T(128)}) custom-call(s32[2]{0:T(128)} %mu_ref.1, s32[2]{0:T(128)} %nu_ref.1, s32[1]{0:T(128)S(6)} %copy.14.live_ref, s32[16,64]{1,0:T(8,128)} %bitcast.4, bf16[64,1024]{1,0:T(8,128)(2,1)} %coeffs_ref.1, s32[1,512]{1,0:T(1,128)} %bitcast.6, s32[1,512]{1,0:T(1,128)} %bitcast.8, bf16[2,64,16384]{2,1,0:T(8,128)(2,1)} %ints_hbm.1), custom_call_target="tpu_custom_call" | custom-call | tf_op jit(solution)/shard_map/exchange/pallas_call | solution.py:532
  68.5 0.0 copy-done
  68.5 0.0 copy-done.5
  68.6 0.0 copy-done.4
  68.6 0.0 copy-done.3
  68.6 0.0 copy-done.2
  68.6 0.0 copy-done.1
  68.6 0.2 conditional.1
  68.8 0.6 copy.15
Async XLA Ops:
  0.0 68.5 %copy-start = (bf16[64,1024]{1,0:T(8,128)(2,1)S(1)}, bf16[64,1024]{1,0:T(8,128)(2,1)}, u32[]{:S(2)}) copy-start(bf16[64,1024]{1,0:T(8,128)(2,1)} %coeffs_ref.1) | copy-start | bytes 393220
  0.0 68.5 %copy-start.5 = (s32[2]{0:T(128)S(1)}, s32[2]{0:T(128)}, u32[]{:S(2)}) copy-start(s32[2]{0:T(128)} %nu_ref.1) | copy-start | bytes 28
  0.0 68.6 %copy-start.4 = (s32[2]{0:T(128)S(1)}, s32[2]{0:T(128)}, u32[]{:S(2)}) copy-start(s32[2]{0:T(128)} %mu_ref.1) | copy-start | bytes 28
  0.0 68.6 %copy-start.3 = (s32[512]{0:T(512)S(1)}, s32[512]{0:T(512)}, u32[]{:S(2)}) copy-start(s32[512]{0:T(512)} %param.17) | copy-start | bytes 6148
  0.0 68.6 %copy-start.2 = (s32[512]{0:T(512)S(1)}, s32[512]{0:T(512)}, u32[]{:S(2)}) copy-start(s32[512]{0:T(512)} %param.16) | copy-start | bytes 6148
  0.0 68.6 %copy-start.1 = (s32[64,16]{0,1:T(8,128)S(1)}, s32[64,16]{0,1:T(8,128)}, u32[]{:S(2)}) copy-start(s32[64,16]{0,1:T(8,128)} %param.14) | copy-start | bytes 12292

commit v6 on v5

--- a/solution.py
+++ b/solution.py
@@ -19,6 +19,7 @@
 QS = 4
 COLS = AUX_DEV * TILE // (QS * N_ORB)
 ROWS = COLS // 128 * OCC
+HALF = TILE // 2
 CAP = 20
 MESH = pl.DeviceIdType.MESH
 VMEM = pl.BlockSpec(memory_space=pltpu.VMEM)
@@ -42,13 +43,17 @@
     mu_ref,
     nu_ref,
     live_ref,
+    support_hbm,
+    coeffs_hbm,
+    pm_hbm,
+    pn_hbm,
+    ints_hbm,
+    out_ref,
+    any_ref,
     support_ref,
     coeffs_ref,
     pm_ref,
     pn_ref,
-    ints_hbm,
-    out_ref,
-    any_ref,
     ints,
     sbuf,
     rbuf,
@@ -83,6 +88,7 @@
     s2_b,
     r2_a,
     r2_b,
+    small_sem,
     in_sem,
     send_sem,
     recv_sem,
@@ -128,6 +134,14 @@
     for axis in "xy":
         for step in STEPS:
             pl.semaphore_signal(barrier, inc=1, device_id=along(axis, step), device_id_type=MESH)
+    small = [
+        pltpu.make_async_copy(source, target, small_sem.at[i])
+        for i, (source, target) in enumerate(
+            ((support_hbm, support_ref), (coeffs_hbm, coeffs_ref), (pm_hbm, pm_ref), (pn_hbm, pn_ref))
+        )
+    ]
+    for copy in small:
+        copy.start()
     for q in range(QS):
         load(q).start()
 
@@ -136,15 +150,19 @@
     one = (
         lax.broadcasted_iota(jnp.int32, (SUP, SUP), 0) == lax.broadcasted_iota(jnp.int32, (SUP, SUP), 1)
     ).astype(jnp.float32)
+    small[0].wait()
     support = lax.dot_general(
         support_ref[...].astype(jnp.float32), one, (((0,), (0,)), ((), ())), preferred_element_type=jnp.float32
     )
+    for j in range(SUP):
+        tiles[j] = jnp.broadcast_to(support[:, j : j + 1], (OCC, 128))
+    small[1].wait()
     halves = []
     for s in range(2):
         total = jnp.zeros((OCC, 128), jnp.float32)
         nu = nu_ref[s].astype(jnp.float32)
         for jj in range(SUP // 2):
-            tile = jnp.where(low, support[:, 2 * jj : 2 * jj + 1], support[:, 2 * jj + 1 : 2 * jj + 2])
+            tile = jnp.where(low, tiles[2 * jj], tiles[2 * jj + 1])
             block = coeffs_ref[:, jj * 128 : (jj + 1) * 128].astype(jnp.float32)
             total = total + jnp.where(tile == nu, block, 0.0)
         total = total + pltpu.roll(total, 64, 1)
@@ -157,8 +175,6 @@
     mine[0] = jnp.where(slot < live_ref[0], jnp.where(slot == 0, mu_ref[0], mu_ref[1]), -1)
     mine[1] = jnp.where(slot < live_ref[0], jnp.where(slot == 0, nu_ref[0], nu_ref[1]), -1)
 
-    for j in range(SUP):
-        tiles[j] = jnp.broadcast_to(support[:, j : j + 1], (OCC, 128))
     square = (2 * OCC, 2 * OCC)
     to, at = lax.broadcasted_iota(jnp.int32, square, 0), lax.broadcasted_iota(jnp.int32, square, 1)
     before = jnp.where(at < to, 1.0, 0.0).astype(jnp.bfloat16)
@@ -201,13 +217,13 @@
             device_id_type=MESH,
         )
 
-    def swap(step):
+    def swap(part, step):
         zz = lax.rem(z + step, 4)
         return pltpu.make_async_remote_copy(
-            src_ref=gsend.at[zz],
-            dst_ref=gpeer.at[zz],
-            send_sem=g_send.at[step],
-            recv_sem=g_recv.at[step],
+            src_ref=gsend.at[part, zz],
+            dst_ref=gpeer.at[part, zz],
+            send_sem=g_send.at[part, step],
+            recv_sem=g_recv.at[part, step],
             device_id=(aux, peer),
             device_id_type=MESH,
         )
@@ -301,6 +317,8 @@
             merged = jnp.concatenate([merged[:, : N_ORB * top], turned], axis=1)
             merge[1, pair // 4, at] = merged.astype(jnp.bfloat16)
 
+    for copy in small[2:]:
+        copy.wait()
     k = lax.broadcasted_iota(jnp.int32, pm_ref.shape, 1)
     u = jnp.full(pm_ref.shape, -1, jnp.int32)
     v = jnp.full(pm_ref.shape, -1, jnp.int32)
@@ -332,7 +350,8 @@
     ]
     for copy in to_smem:
         copy.start()
-    blocks[cap // 2] = jnp.zeros((TILE, 128), jnp.bfloat16)
+    for part in range(2):
+        blocks[part, cap // 2] = jnp.zeros((HALF, 128), jnp.bfloat16)
 
     tell_x = tell(0, "x", over)
     for copy in tell_x:
@@ -393,111 +412,115 @@
         copy.wait()
 
     def ring(part, stage, axis, source, landing, step):
-        at = part * 2 + stage
-        return pltpu.make_async_remote_copy(
-            src_ref=source.at[lax.rem(place[axis] + step, 4)],
-            dst_ref=landing.at[3 - step],
+        at = part * 5 + stage
+        copy = pltpu.make_async_remote_copy(
+            src_ref=source.at[part, lax.rem(place[axis] + step, 4)],
+            dst_ref=landing.at[part, 3 - step],
             send_sem=ring_send.at[at, step - 1],
             recv_sem=ring_recv.at[at, 3 - step],
             device_id=along(axis, step),
             device_id_type=MESH,
         )
-
-    def started(copy):
         copy.start()
         return copy
 
-    def packed_tiles(owner, b):
+    low = low[:HALF]
+
+    def packed_tiles(part, owner, b):
         at = owner * cap + 2 * b
         t0, t1 = order_smem[0, at] & 255, order_smem[0, at + 1] & 255
-        tile0, tile1 = acc[t0 >> 1], acc[t1 >> 1]
+        rows = slice(part * HALF, (part + 1) * HALF)
+        tile0, tile1 = acc[t0 >> 1, rows], acc[t1 >> 1, rows]
         in_place = jnp.broadcast_to(jnp.where(low_row, t0 & 1, 1 - (t1 & 1)), low.shape) == 0
         straight, crossed = jnp.where(low, tile0, tile1), jnp.where(low, tile1, tile0)
         return jnp.where(in_place, straight, pltpu.roll(crossed, 64, 1))
 
     unroll = 10 if cap % 10 == 0 else 4
 
-    def give(step):
+    def give(part, step):
         zz = lax.rem(z + step, 4)
 
         @pl.loop(0, cap // 2, unroll=unroll)
         def _(b):
-            gsend[zz, b] = packed_tiles(zz * 2 + 1 - core, b).astype(jnp.bfloat16)
-
-        swap(step).start()
-
-    z_copies = []
-
-    def take(step):
+            gsend[part, zz, b] = packed_tiles(part, zz * 2 + 1 - core, b).astype(jnp.bfloat16)
+
+        swap(part, step).start()
+
+    z_copies = ([], [])
+
+    def take(part, step):
         zz = lax.rem(z + step, 4)
 
         @pl.loop(0, cap // 2, unroll=unroll)
         def _(b):
-            kept_tiles[b] = packed_tiles(zz * 2 + core, b)
-
-        swap(step).wait_recv()
-        sz[zz] = (kept_tiles[...] + gpeer[zz].astype(jnp.float32)).astype(jnp.bfloat16)
+            kept_tiles[b] = packed_tiles(part, zz * 2 + core, b)
+
+        swap(part, step).wait_recv()
+        sz[part, zz] = (kept_tiles[...] + gpeer[part, zz].astype(jnp.float32)).astype(jnp.bfloat16)
         if step:
-            z_copies.append(started(ring(2, 0, "z", sz, rz, step)))
+            z_copies[part].append(ring(part, 0, "z", sz, rz, step))
 
     turns = STEPS + (0,)
-    give(turns[0])
-    for i in range(4):
-        if i < 3:
-            give(turns[i + 1])
-        take(turns[i])
-
-    for copy in z_copies:
-        copy.wait_recv()
-    for b in range(cap // 2):
-        total = sz[z, b].astype(jnp.float32)
-        for n in range(3):
-            total = total + rz[n, b].astype(jnp.float32)
-        blocks[b] = total.astype(jnp.bfloat16)
-        blocks[cap // 2 + 1 + b] = pltpu.roll(total, 64, 1).astype(jnp.bfloat16)
-
-    def block(yy, xx, j):
+    todo = [(part, step) for part in range(2) for step in turns]
+    give(*todo[0])
+    for i in range(8):
+        if i < 7:
+            give(*todo[i + 1])
+        take(*todo[i])
+
+    def block(part, yy, xx, j):
         k = (yy * 4 + xx) * 32 + z * 8 + core * 4 + 2 * j
         left, right = (jnp.clip(index_smem[0, k + h], 0, cap + 1) for h in range(2))
-        return jnp.where(low, blocks[left], blocks[right])
-
-    one_a, one_b = [], []
-    for step in turns:
-        xx, yy = lax.rem(x + step, 4), lax.rem(y + step, 4)
-        for i in range(4):
-            e_a[xx, i] = block(i, xx, 0)
-        if step:
-            one_a.append(started(ring(0, 0, "x", e_a, r1_a, step)))
-        for i in range(4):
-            e_b[yy, i] = block(yy, i, 1)
-        if step:
-            one_b.append(started(ring(1, 0, "y", e_b, r1_b, step)))
-
-    two = []
-    for part, copies, axis, then, e, r1, s2, r2 in (
-        (0, one_a, "x", "y", e_a, r1_a, s2_a, r2_a),
-        (1, one_b, "y", "x", e_b, r1_b, s2_b, r2_b),
-    ):
-        for copy in copies:
+        return jnp.where(low, blocks[part, left], blocks[part, right])
+
+    one_a, one_b, two_a, two_b = ([], []), ([], []), ([], []), ([], [])
+    for part in range(2):
+        for copy in z_copies[part]:
             copy.wait_recv()
+        for b in range(cap // 2):
+            total = sz[part, z, b].astype(jnp.float32)
+            for n in range(3):
+                total = total + rz[part, n, b].astype(jnp.float32)
+            blocks[part, b] = total.astype(jnp.bfloat16)
+            blocks[part, cap // 2 + 1 + b] = pltpu.roll(total, 64, 1).astype(jnp.bfloat16)
         for step in turns:
-            i = lax.rem(place[then] + step, 4)
-            total = e[place[axis], i].astype(jnp.float32)
-            for n in range(3):
-                total = total + r1[n, i].astype(jnp.float32)
-            s2[i] = total
+            xx, yy = lax.rem(x + step, 4), lax.rem(y + step, 4)
+            for i in range(4):
+                e_a[part, xx, i] = block(part, i, xx, 0)
             if step:
-                two.append(started(ring(part, 1, then, s2, r2, step)))
+                one_a[part].append(ring(part, 1, "x", e_a, r1_a, step))
+            for i in range(4):
+                e_b[part, yy, i] = block(part, yy, i, 1)
+            if step:
+                one_b[part].append(ring(part, 2, "y", e_b, r1_b, step))
+
+    for part in range(2):
+        for stage, copies, more, axis, then, e, r1, s2, r2 in (
+            (3, one_a, two_a, "x", "y", e_a, r1_a, s2_a, r2_a),
+            (4, one_b, two_b, "y", "x", e_b, r1_b, s2_b, r2_b),
+        ):
+            for copy in copies[part]:
+                copy.wait_recv()
+            for step in turns:
+                i = lax.rem(place[then] + step, 4)
+                total = e[part, place[axis], i].astype(jnp.float32)
+                for n in range(3):
+                    total = total + r1[part, n, i].astype(jnp.float32)
+                s2[part, i] = total
+                if step:
+                    more[part].append(ring(part, stage, then, s2, r2, step))
 
     for copy in tell_y:
         copy.wait_recv()
     found = jnp.max(row[...] + overs[1, 0] + overs[1, 1] + overs[1, 2])
     any_ref[0] = jnp.where(found > 0.5, 1, 0)
 
-    for part, then, s2, r2 in ((0, "y", s2_a, r2_a), (1, "x", s2_b, r2_b)):
-        for copy in two[part * 3 : part * 3 + 3]:
-            copy.wait_recv()
-        done[part] = s2[place[then]] + r2[0] + r2[1] + r2[2]
+    for part in range(2):
+        rows = slice(part * HALF, (part + 1) * HALF)
+        for j, copies, then, s2, r2 in ((0, two_a, "y", s2_a, r2_a), (1, two_b, "x", s2_b, r2_b)):
+            for copy in copies[part]:
+                copy.wait_recv()
+            done[j, rows] = s2[part, place[then]] + r2[part, 0] + r2[part, 1] + r2[part, 2]
     low = lax.broadcasted_iota(jnp.int32, (TILE // 2, 128), 1) < TILE
     for i in range(2):
         even = done[i, pl.ds(0, TILE // 2, stride=2), :]
@@ -508,10 +531,12 @@
             out_ref[2 * i : 2 * i + 1, m * 128 : (m + 1) * 128] = left[m : m + 1]
             out_ref[2 * i + 1 : 2 * i + 2, m * 128 : (m + 1) * 128] = right[m : m + 1]
 
-    for copy in z_copies + one_a + one_b + two + tell_x + tell_y:
-        copy.wait_send()
-    for step in range(4):
-        swap(step).wait_send()
+    for copies in (*z_copies, *one_a, *one_b, *two_a, *two_b, tell_x, tell_y):
+        for copy in copies:
+            copy.wait_send()
+    for part in range(2):
+        for step in range(4):
+            swap(part, step).wait_send()
     for t in range(len(others)):
         mu_copy(t, me).wait_send()
 
@@ -535,9 +560,10 @@
             jax.ShapeDtypeStruct((4, TILE * TILE), f32),
             jax.ShapeDtypeStruct((1,), jnp.int32),
         ),
-        in_specs=[SMEM] * 3 + [VMEM] * 4 + [pl.BlockSpec(memory_space=pl.ANY)],
+        in_specs=[SMEM] * 3 + [pl.BlockSpec(memory_space=pl.ANY)] * 5,
         out_specs=(VMEM, SMEM),
         scratch_shapes=[
+            *(pltpu.VMEM(array.shape, array.dtype) for array in (support, coeffs, pair_mu, pair_nu)),
             pltpu.VMEM((QS, 2, TILE, COLS * N_ORB), bf16),
             pltpu.VMEM((QS, N_ORB - 1, rows, 128), bf16),
             pltpu.VMEM((QS, N_ORB, rows, 128), bf16),
@@ -558,33 +584,34 @@
             pltpu.VMEM((8, 128), f32),
             pltpu.VMEM((2, 3, 8, 128), f32),
             pltpu.VMEM((2, TILE, 128), f32),
-            pltpu.VMEM((4, half, TILE, 128), bf16),
-            pltpu.VMEM((4, half, TILE, 128), bf16),
-            pltpu.VMEM((half, TILE, 128), f32),
-            pltpu.VMEM((4, half, TILE, 128), bf16),
-            pltpu.VMEM((3, half, TILE, 128), bf16),
-            pltpu.VMEM((cap + 2, TILE, 128), bf16),
-            pltpu.VMEM((4, 4, TILE, 128), bf16),
-            pltpu.VMEM((4, 4, TILE, 128), bf16),
-            pltpu.VMEM((3, 4, TILE, 128), bf16),
-            pltpu.VMEM((3, 4, TILE, 128), bf16),
-            pltpu.VMEM((4, TILE, 128), f32),
-            pltpu.VMEM((4, TILE, 128), f32),
-            pltpu.VMEM((3, TILE, 128), f32),
-            pltpu.VMEM((3, TILE, 128), f32),
+            pltpu.VMEM((2, 4, half, HALF, 128), bf16),
+            pltpu.VMEM((2, 4, half, HALF, 128), bf16),
+            pltpu.VMEM((half, HALF, 128), f32),
+            pltpu.VMEM((2, 4, half, HALF, 128), bf16),
+            pltpu.VMEM((2, 3, half, HALF, 128), bf16),
+            pltpu.VMEM((2, cap + 2, HALF, 128), bf16),
+            pltpu.VMEM((2, 4, 4, HALF, 128), bf16),
+            pltpu.VMEM((2, 4, 4, HALF, 128), bf16),
+            pltpu.VMEM((2, 3, 4, HALF, 128), bf16),
+            pltpu.VMEM((2, 3, 4, HALF, 128), bf16),
+            pltpu.VMEM((2, 4, HALF, 128), f32),
+            pltpu.VMEM((2, 4, HALF, 128), f32),
+            pltpu.VMEM((2, 3, HALF, 128), f32),
+            pltpu.VMEM((2, 3, HALF, 128), f32),
+            dma((4,)),
             dma((QS,)),
             dma((QS, N_ORB - 1)),
             dma((QS, N_ORB)),
             dma((N_ORB - 1,)),
             dma((N_ORB,)),
-            dma((4,)),
-            dma((4,)),
+            dma((2, 4)),
+            dma((2, 4)),
             dma(()),
             dma(()),
             dma((2, 3)),
             dma((2, 3)),
-            dma((5, 3)),
-            dma((5, 3)),
+            dma((10, 3)),
+            dma((10, 3)),
         ],
         compiler_params=pltpu.CompilerParams(
             collective_id=identity, has_side_effects=True, vmem_limit_bytes=LIMIT

time: 69.6 us -> 68.2 us (0.980)
  Pallas kernels: 67.2 us -> 65.8 us
    pallas_call x1, Pallas kernels: 67.2 us -> 65.8 us  [exchange(): pl.pallas_call(functools.partial(exchange_kernel, pool, cap), out_shape=(...]
where the time goes in v6:
time: 68.2 us; the launch traced here: 68 us
  Pallas kernels  65.8 us (96%)
  between operations  1.39 us (2%)
    pallas_call x1, Pallas kernels, exchange(): pl.pallas_call(functools.partial(exchange_kernel, pool, cap), out_shape=(...  65.8 us

profile of v6, /device:TPU:0, one launch (start us, length us, event | category | flops | bytes accessed | tf_op | source)
XLA Modules:
  0.0 68.0 jit_solution(13629698728163012473)
XLA Ops:
  0.0 0.0 copy-start
  0.0 0.0 copy-start.5
  0.0 0.0 copy-start.4
  0.0 0.0 copy-start.3
  0.0 0.0 copy-start.2
  0.0 0.0 copy-start.1
  0.7 65.8 %exchange.3 = (f32[4,4096]{1,0:T(4,128)S(1)}, s32[1]{0:T(128)}) custom-call(s32[2]{0:T(128)} %mu_ref.1, s32[2]{0:T(128)} %nu_ref.1, s32[1]{0:T(128)S(6)} %copy.14.live_ref, s32[16,64]{1,0:T(8,128)} %bitcast.4, bf16[64,1024]{1,0:T(8,128)(2,1)} %coeffs_hbm.1, s32[1,512]{1,0:T(1,128)} %bitcast.6, s32[1,512]{1,0:T(1,128)} %bitcast.8, bf16[2,64,16384]{2,1,0:T(8,128)(2,1)} %ints_hbm.1), custom_call_target="tpu_custom_call" | custom-call | tf_op jit(solution)/shard_map/exchange/pallas_call | solution.py:557
  67.1 0.0 copy-done
  67.1 0.0 copy-done.5
  67.2 0.0 copy-done.4
  67.2 0.0 copy-done.3
  67.2 0.0 copy-done.2
  67.2 0.0 copy-done.1
  67.2 0.2 conditional.1
  67.4 0.6 copy.15
Async XLA Ops:
  0.0 67.1 %copy-start = (bf16[64,1024]{1,0:T(8,128)(2,1)S(1)}, bf16[64,1024]{1,0:T(8,128)(2,1)}, u32[]{:S(2)}) copy-start(bf16[64,1024]{1,0:T(8,128)(2,1)} %coeffs_hbm.1) | copy-start | bytes 393220
  0.0 67.1 %copy-start.5 = (s32[2]{0:T(128)S(1)}, s32[2]{0:T(128)}, u32[]{:S(2)}) copy-start(s32[2]{0:T(128)} %nu_ref.1) | copy-start | bytes 28
  0.0 67.2 %copy-start.4 = (s32[2]{0:T(128)S(1)}, s32[2]{0:T(128)}, u32[]{:S(2)}) copy-start(s32[2]{0:T(128)} %mu_ref.1) | copy-start | bytes 28
  0.0 67.2 %copy-start.3 = (s32[512]{0:T(512)S(1)}, s32[512]{0:T(512)}, u32[]{:S(2)}) copy-start(s32[512]{0:T(512)} %param.17) | copy-start | bytes 6148
  0.0 67.2 %copy-start.2 = (s32[512]{0:T(512)S(1)}, s32[512]{0:T(512)}, u32[]{:S(2)}) copy-start(s32[512]{0:T(512)} %param.16) | copy-start | bytes 6148
  0.0 67.2 %copy-start.1 = (s32[64,16]{0,1:T(8,128)S(1)}, s32[64,16]{0,1:T(8,128)}, u32[]{:S(2)}) copy-start(s32[64,16]{0,1:T(8,128)} %param.14) | copy-start | bytes 12292

commit v7 on v6

--- a/solution.py
+++ b/solution.py
@@ -42,7 +42,7 @@
     cap,
     mu_ref,
     nu_ref,
-    live_ref,
+    live_hbm,
     support_hbm,
     coeffs_hbm,
     pm_hbm,
@@ -50,6 +50,7 @@
     ints_hbm,
     out_ref,
     any_ref,
+    live_ref,
     support_ref,
     coeffs_ref,
     pm_ref,
@@ -137,7 +138,13 @@
     small = [
         pltpu.make_async_copy(source, target, small_sem.at[i])
         for i, (source, target) in enumerate(
-            ((support_hbm, support_ref), (coeffs_hbm, coeffs_ref), (pm_hbm, pm_ref), (pn_hbm, pn_ref))
+            (
+                (support_hbm, support_ref),
+                (coeffs_hbm, coeffs_ref),
+                (live_hbm, live_ref),
+                (pm_hbm, pm_ref),
+                (pn_hbm, pn_ref),
+            )
         )
     ]
     for copy in small:
@@ -157,6 +164,7 @@
     for j in range(SUP):
         tiles[j] = jnp.broadcast_to(support[:, j : j + 1], (OCC, 128))
     small[1].wait()
+    small[2].wait()
     halves = []
     for s in range(2):
         total = jnp.zeros((OCC, 128), jnp.float32)
@@ -317,7 +325,7 @@
             merged = jnp.concatenate([merged[:, : N_ORB * top], turned], axis=1)
             merge[1, pair // 4, at] = merged.astype(jnp.bfloat16)
 
-    for copy in small[2:]:
+    for copy in small[3:]:
         copy.wait()
     k = lax.broadcasted_iota(jnp.int32, pm_ref.shape, 1)
     u = jnp.full(pm_ref.shape, -1, jnp.int32)
@@ -560,9 +568,10 @@
             jax.ShapeDtypeStruct((4, TILE * TILE), f32),
             jax.ShapeDtypeStruct((1,), jnp.int32),
         ),
-        in_specs=[SMEM] * 3 + [pl.BlockSpec(memory_space=pl.ANY)] * 5,
+        in_specs=[SMEM] * 2 + [pl.BlockSpec(memory_space=pl.ANY)] * 6,
         out_specs=(VMEM, SMEM),
         scratch_shapes=[
+            pltpu.SMEM(live.shape, live.dtype),
             *(pltpu.VMEM(array.shape, array.dtype) for array in (support, coeffs, pair_mu, pair_nu)),
             pltpu.VMEM((QS, 2, TILE, COLS * N_ORB), bf16),
             pltpu.VMEM((QS, N_ORB - 1, rows, 128), bf16),
@@ -598,7 +607,7 @@
             pltpu.VMEM((2, 4, HALF, 128), f32),
             pltpu.VMEM((2, 3, HALF, 128), f32),
             pltpu.VMEM((2, 3, HALF, 128), f32),
-            dma((4,)),
+            dma((5,)),
             dma((QS,)),
             dma((QS, N_ORB - 1)),
             dma((QS, N_ORB)),
@@ -624,7 +633,7 @@
     args = (tile_mu, tile_nu, live_count, support.T, coeffs, pair_mu[None, :], pair_nu[None, :], integrals)
 
     out, over = exchange(POOL, CAP, 0, *args)
-    return lax.cond(over[0] == 0, lambda: out, lambda: exchange(2 * OCC, NPAIR // N_ORB, 1, *args)[0])
+    return lax.switch(over[0], (lambda: out, lambda: exchange(2 * OCC, NPAIR // N_ORB, 1, *args)[0]))
 
 
 def solution(mesh):

time: 68.2 us -> 68.2 us (level)
  no operation moved by 1% of the time
where the time goes in v7:
time: 68.2 us; the launch traced here: 68 us
  Pallas kernels  65.8 us (96%)
  between operations  1.39 us (2%)
    pallas_call x1, Pallas kernels, exchange(): pl.pallas_call(functools.partial(exchange_kernel, pool, cap), out_shape=(...  65.8 us

profile of v7, /device:TPU:0, one launch (start us, length us, event | category | flops | bytes accessed | tf_op | source)
XLA Modules:
  0.0 68.0 jit_solution(3840446932854685836)
XLA Ops:
  0.0 0.0 copy-start
  0.0 0.0 copy-start.5
  0.0 0.0 copy-start.4
  0.0 0.0 copy-start.3
  0.0 0.0 copy-start.2
  0.0 0.0 copy-start.1
  0.7 65.8 %exchange.3 = (f32[4,4096]{1,0:T(4,128)S(1)}, s32[1]{0:T(128)}) custom-call(s32[2]{0:T(128)} %mu_ref.1, s32[2]{0:T(128)} %nu_ref.1, s32[1]{0:T(128)S(6)} %copy.14.live_hbm, s32[16,64]{1,0:T(8,128)} %bitcast.4, bf16[64,1024]{1,0:T(8,128)(2,1)} %coeffs_hbm.1, s32[1,512]{1,0:T(1,128)} %bitcast.6, s32[1,512]{1,0:T(1,128)} %bitcast.8, bf16[2,64,16384]{2,1,0:T(8,128)(2,1)} %ints_hbm.1), custom_call_target="tpu_custom_call" | custom-call | tf_op jit(solution)/shard_map/exchange/pallas_call | solution.py:565
  67.2 0.0 copy-done
  67.2 0.0 copy-done.5
  67.2 0.0 copy-done.4
  67.2 0.0 copy-done.3
  67.2 0.0 copy-done.2
  67.2 0.0 copy-done.1
  67.2 0.2 conditional.1
  67.4 0.6 copy.15
Async XLA Ops:
  0.0 67.2 %copy-start = (bf16[64,1024]{1,0:T(8,128)(2,1)S(1)}, bf16[64,1024]{1,0:T(8,128)(2,1)}, u32[]{:S(2)}) copy-start(bf16[64,1024]{1,0:T(8,128)(2,1)} %coeffs_hbm.1) | copy-start | bytes 393220
  0.0 67.2 %copy-start.5 = (s32[2]{0:T(128)S(1)}, s32[2]{0:T(128)}, u32[]{:S(2)}) copy-start(s32[2]{0:T(128)} %nu_ref.1) | copy-start | bytes 28
  0.0 67.2 %copy-start.4 = (s32[2]{0:T(128)S(1)}, s32[2]{0:T(128)}, u32[]{:S(2)}) copy-start(s32[2]{0:T(128)} %mu_ref.1) | copy-start | bytes 28
  0.0 67.2 %copy-start.3 = (s32[512]{0:T(512)S(1)}, s32[512]{0:T(512)}, u32[]{:S(2)}) copy-start(s32[512]{0:T(512)} %param.17) | copy-start | bytes 6148
  0.0 67.2 %copy-start.2 = (s32[512]{0:T(512)S(1)}, s32[512]{0:T(512)}, u32[]{:S(2)}) copy-start(s32[512]{0:T(512)} %param.16) | copy-start | bytes 6148
  0.0 67.2 %copy-start.1 = (s32[64,16]{0,1:T(8,128)S(1)}, s32[64,16]{0,1:T(8,128)}, u32[]{:S(2)}) copy-start(s32[64,16]{0,1:T(8,128)} %param.14) | copy-start | bytes 12292
